TPU v7x, 32 devices: a whole 2x2x4 slice. The times are simulated.
32 devices in a mesh: cfg: 2 (over core), seq: 16 (over z, y, x).
Axes of the slice: x: 2, y: 2, z: 4, core: 2. Of those that a mesh axis runs over, the one named last changes fastest.
Arguments:
- queries: bfloat16 [2, 512, 2432], P('cfg', 'seq'), may hold values from -6 to 6
- image_keys: bfloat16 [2, 512, 2432], P('cfg', 'seq'), may hold values from -6 to 6
- image_values: bfloat16 [2, 512, 2432], P('cfg', 'seq'), may hold values from -6 to 6
- text_keys: bfloat16 [2, 64, 2432], P('cfg', 'seq'), may hold values from -6 to 6
- text_values: bfloat16 [2, 64, 2432], P('cfg', 'seq'), may hold values from -6 to 6
- hidden_in: bfloat16 [2, 512, 2432], P('cfg', 'seq'), may hold values from -6 to 6
- modulation: float32 [2, 6, 2432], P('cfg'), may hold values from 0.25 to 1.75
- w_out: bfloat16 [2432, 2432], replicated, may hold values from -0.125 to 0.125
- w_up: bfloat16 [2432, 9728], P(None, 'seq'), may hold values from -0.125 to 0.125
- w_down: bfloat16 [9728, 2432], P('seq'), may hold values from -0.0625 to 0.0625
- w_final: bfloat16 [2432, 64], replicated, may hold values from -0.125 to 0.125
- latent: float32 [512, 64], P('seq', 'cfg'), may hold values from -6 to 6
- text_len: int32 [2], P('cfg'), may hold values from 8 to 64, as said below
- step_index: int32 [1], replicated, may hold values from 0 to 26
- guidance: float32 [1], replicated, may hold values from 3.5 to 7
Outputs:
- velocity: float32 [512, 64], P('seq', 'cfg')
- next_latent: float32 [512, 64], P('seq', 'cfg')
Inputs may be any that keep to these rules, and one draw needn't show every extreme that they name: `text_len`: in every draw one of the two halves has exactly 64 valid text tokens.
All inputs are finite; a program needn't handle non-finite values.
Results may differ from a plain program's by a relative error of at most 0.0095.
Values may be sent and summed in bfloat16 or wider, within the bound.
A program may use at most 128 MiB of HBM per device.

v0:
```python
import jax
import jax.numpy as jnp
from jax import lax
from jax.sharding import PartitionSpec as P

HEADS = 38
HEAD_DIM = 64
STEPS = 28


shift_value = 3.0
norm_eps = 1e-06


def partner_2(value, axis, bit):
    mask = 2**bit
    pairs = [(source, source ^ mask) for source in range(lax.axis_size(axis))]
    return lax.ppermute(value, axis, pairs)


def layer_norm(values):
    centred = values - jnp.mean(values, -1, keepdims=True)
    return centred / jnp.sqrt(jnp.mean(centred * centred, -1, keepdims=True) + norm_eps)


def sigma_at(index):
    frac = 1.0 - index.astype(jnp.float32) / STEPS
    return shift_value * frac / (1.0 + (shift_value - 1.0) * frac)


def body(
    queries,
    image_keys,
    image_values,
    text_keys,
    text_values,
    hidden_in,
    modulation,
    w_out,
    w_up,
    w_down,
    w_final,
    latent,
    text_len,
    step_index,
    guidance,
):
    img_rows = queries.shape[1]
    text_rows = text_keys.shape[1]
    both_rows = img_rows + text_rows
    width = queries.shape[2]
    length = text_len[0]
    score_scale = HEAD_DIM ** (-0.5)
    key_rows = jnp.concatenate([image_keys[0], text_keys[0]], 0)
    value_rows = jnp.concatenate([image_values[0], text_values[0]], 0)
    seq_count = lax.axis_size("seq")
    img_all = img_rows * seq_count
    unit_count = HEADS * img_rows
    head_span = min(HEADS, (unit_count - 1) // img_all + 2)
    slot_width = head_span * HEAD_DIM
    targets = jnp.arange(seq_count, dtype=jnp.int32)
    first_head = targets * unit_count // img_all
    slot_heads = first_head[:, None] + jnp.arange(head_span, dtype=jnp.int32)[None, :]
    head_pick = jnp.minimum(slot_heads, HEADS - 1).reshape(-1)

    def spread(rows):
        count = rows.shape[0]
        return jnp.take(rows.reshape(count, HEADS, HEAD_DIM), head_pick, axis=1).reshape(
            count, seq_count, slot_width
        )

    query_in, key_in, value_in = (
        lax.all_to_all(spread(queries[0]), "seq", split_axis=1, concat_axis=1, tiled=True),
        lax.all_to_all(spread(key_rows), "seq", split_axis=1, concat_axis=1, tiled=True),
        lax.all_to_all(spread(value_rows), "seq", split_axis=1, concat_axis=1, tiled=True),
    )
    myself = lax.axis_index("seq")
    lead = myself * unit_count // img_all
    offset = myself * unit_count - lead * img_all
    query_flat = (
        query_in.reshape(img_rows, seq_count, head_span, HEAD_DIM)
        .transpose(2, 1, 0, 3)
        .reshape(head_span * img_all, HEAD_DIM)
    )
    query_units = lax.dynamic_slice_in_dim(query_flat, offset, unit_count, 0)
    unit_slot = (offset + jnp.arange(unit_count, dtype=jnp.int32)) // img_all
    slot_match = unit_slot[:, None] == jnp.arange(head_span, dtype=jnp.int32)[None, :]
    query_wide = jnp.where(
        slot_match[:, :, None], query_units[:, None, :], jnp.zeros((), jnp.bfloat16)
    ).reshape(unit_count, slot_width)
    key_count = both_rows * seq_count
    key_all = key_in.reshape(key_count, slot_width)
    value_all = value_in.reshape(key_count, slot_width)
    scores = (
        jnp.einsum("uw,kw->uk", query_wide, key_all, preferred_element_type=jnp.float32)
        * score_scale
    )
    local_row = jnp.arange(both_rows, dtype=jnp.int32)[:, None]
    text_slot = targets[None, :] * text_rows + local_row - img_rows
    valid = ((local_row < img_rows) | (text_slot < length)).reshape(-1)
    scores = jnp.where(valid[None, :], scores, -1e30)
    row_top = jnp.max(scores, -1, keepdims=True)
    weights = jnp.exp(scores - row_top)
    total = jnp.sum(weights, -1, keepdims=True)
    mixed = jnp.dot(
        weights.astype(jnp.bfloat16), value_all, preferred_element_type=jnp.float32
    ).reshape(unit_count, head_span, HEAD_DIM)
    picked = jnp.sum(jnp.where(slot_match[:, :, None], mixed, 0.0), 1)
    unit_out = (picked / total).astype(jnp.bfloat16)
    placed = lax.dynamic_update_slice_in_dim(
        jnp.zeros((head_span * img_all, HEAD_DIM), jnp.bfloat16), unit_out, offset, 0
    )
    going = (
        placed.reshape(head_span, seq_count, img_rows, HEAD_DIM)
        .transpose(2, 1, 0, 3)
        .reshape(img_rows, seq_count, slot_width)
    )
    coming = lax.all_to_all(going, "seq", split_axis=1, concat_axis=1, tiled=True)
    owner = (slot_heads[:, :, None] == jnp.arange(HEADS, dtype=jnp.int32)[None, None, :]).astype(
        jnp.bfloat16
    )
    attended = (
        jnp.einsum(
            "rjsd,jsh->rhd",
            coming.reshape(img_rows, seq_count, head_span, HEAD_DIM),
            owner,
            preferred_element_type=jnp.float32,
        )
        .reshape(img_rows, width)
        .astype(jnp.bfloat16)
    )
    mods = modulation[0]
    projected = jnp.dot(attended, w_out, preferred_element_type=jnp.float32)
    middle = hidden_in[0].astype(jnp.float32) + mods[0] * projected
    normed = (layer_norm(middle) * (1.0 + mods[2]) + mods[1]).astype(jnp.bfloat16)
    hidden_all = jax.nn.gelu(
        jnp.dot(
            lax.all_gather(normed, "seq", axis=0, tiled=True),
            w_up,
            preferred_element_type=jnp.float32,
        ),
        approximate=True,
    ).astype(jnp.bfloat16)
    mlp_out = lax.psum_scatter(
        jnp.dot(hidden_all, w_down, preferred_element_type=jnp.float32),
        "seq",
        scatter_dimension=0,
        tiled=True,
    )
    final = middle + mods[3] * mlp_out
    head_in = (layer_norm(final) * (1.0 + mods[5]) + mods[4]).astype(jnp.bfloat16)
    own_velocity = jnp.dot(head_in, w_final, preferred_element_type=jnp.float32)
    step_size = sigma_at(step_index[0] + 1) - sigma_at(step_index[0])
    scale_now = guidance[0]
    half_width = latent.shape[1]
    partner = partner_2(own_velocity, "cfg", 0)
    is_cond = lax.axis_index("cfg") == 0
    cond_part = jnp.where(is_cond, own_velocity, partner)
    uncond_part = jnp.where(is_cond, partner, own_velocity)
    velocity_full = uncond_part + scale_now * (cond_part - uncond_part)
    velocity = lax.dynamic_slice_in_dim(
        velocity_full, lax.axis_index("cfg") * half_width, half_width, 1
    )
    next_latent = latent + step_size * velocity
    return (velocity, next_latent)


def solution(mesh):
    in_specs = (
        P("cfg", "seq", None),
        P("cfg", "seq", None),
        P("cfg", "seq", None),
        P("cfg", "seq", None),
        P("cfg", "seq", None),
        P("cfg", "seq", None),
        P("cfg", None, None),
        P(),
        P(None, "seq"),
        P("seq", None),
        P(),
        P("seq", "cfg"),
        P("cfg"),
        P(),
        P(),
    )
    out_specs = (P("seq", "cfg"), P("seq", "cfg"))
    return jax.shard_map(body, mesh=mesh, in_specs=in_specs, out_specs=out_specs, check_vma=False)
```

profile of v0, /device:TPU:1, one launch (start us, length us, event | category | flops | bytes accessed | tf_op | source)
XLA Modules:
  0.0 299.1 jit_solution(3099955608573592486)
XLA Ops:
  8.1 1.9 reshape_squeeze.3
  11.0 1.4 gather_fusion
  12.4 1.2 copy.67
  16.6 7.5 %all-to-all-start = ((bf16[32,16,256]{2,0,1:T(8,128)(2,1)}), bf16[32,16,256]{2,0,1:T(8,128)(2,1)}, u32[]{:S(2)}, u32[]{:S(2)}) async-start(bf16[32,16,256]{2,0,1:T(8,128)(2,1)} %copy.68), calls=%async_computation | async-start | bytes 524288 | tf_op jit(solution)/shard_map/all_to_all | solution.py:73
  24.2 1.2 concatenate.16
  30.0 1.5 gather_fusion.1
  32.5 1.5 gather_fusion.2
  34.0 2.5 select_bitcast_fusion.1
  36.6 1.2 copy.74
  38.9 1.8 copy.75
  41.5 1.2 copy.79
  43.8 1.8 copy.80
  45.6 6.3 %all-to-all-start.2 = ((bf16[36,16,256]{2,0,1:T(8,128)(2,1)}), bf16[36,16,256]{2,0,1:T(8,128)(2,1)}, u32[]{:S(2)}, u32[]{:S(2)}) async-start(bf16[36,16,256]{2,0,1:T(8,128)(2,1)} %copy.80), calls=%async_computation.2 | async-start | bytes 655360 | tf_op jit(solution)/shard_map/all_to_all | solution.py:75
  52.0 1.8 copy.69
  53.8 1.2 reshape.301
  56.2 4.3 %all-to-all-done.2 = bf16[36,16,256]{2,0,1:T(8,128)(2,1)} async-done(((bf16[36,16,256]{2,0,1:T(8,128)(2,1)}), bf16[36,16,256]{2,0,1:T(8,128)(2,1)}, u32[]{:S(2)}, u32[]{:S(2)}) %all-to-all-start.2) | async-done | bytes 294944 | tf_op jit(solution)/shard_map/all_to_all | solution.py:75
  60.5 5.5 %all-to-all-start.1 = ((bf16[36,16,256]{2,0,1:T(8,128)(2,1)}), bf16[36,16,256]{2,0,1:T(8,128)(2,1)S(1)}, u32[]{:S(2)}, u32[]{:S(2)}) async-start(bf16[36,16,256]{2,0,1:T(8,128)(2,1)} %copy.75), calls=%async_computation.1 | async-start | bytes 655360 | tf_op jit(solution)/shard_map/all_to_all | solution.py:74
  66.0 1.7 constant_dynamic-slice_fusion
  69.7 1.7 copy.81
  71.5 1.9 copy.82
  74.2 1.7 fusion.41
  79.1 5.8 %all-to-all-start.3 = ((bf16[32,16,256]{2,0,1:T(8,128)(2,1)}), bf16[32,16,256]{2,0,1:T(8,128)(2,1)}, u32[]{:S(2)}, u32[]{:S(2)}) async-start(bf16[32,16,256]{2,0,1:T(8,128)(2,1)} %reshape.355), calls=%async_computation.3 | async-start | bytes 524288 | tf_op jit(solution)/shard_map/all_to_all | solution.py:118
  86.3 5.9 %all-to-all-done.3 = bf16[32,16,256]{2,0,1:T(8,128)(2,1)} async-done(((bf16[32,16,256]{2,0,1:T(8,128)(2,1)}), bf16[32,16,256]{2,0,1:T(8,128)(2,1)}, u32[]{:S(2)}, u32[]{:S(2)}) %all-to-all-start.3) | async-done | bytes 262176 | tf_op jit(solution)/shard_map/all_to_all | solution.py:118
  92.3 1.2 reshape.356
  93.5 1.9 fusion.19
  95.4 1.2 convert_element_type.45
  96.6 6.3 %fusion.42 = (f32[32]{0:T(128)S(1)}, f32[32,2432]{1,0:T(8,128)S(1)}) fusion(bf16[32,2432]{1,0:T(8,128)(2,1)S(1)} %convert_element_type.45, bf16[2432,2432]{1,0:T(8,128)(2,1)} %param.24, f32[2432]{0:T(1024)} %get-tuple-element.7, bf16[1,32,2432]{2,1,0:T(8,128)(2,1)} %param.22), kind=kOutput, calls=%fused_computation.96 | convolution fusion | flops 378847200 | bytes 12461696 | tf_op jit(solution)/shard_map/dot_general | solution.py:133
  104.3 63.5 %all-gather.2.cloned.1.call-done = bf16[512,2432]{1,0:T(8,128)(2,1)} async-done(((bf16[32,2432]{1,0:T(8,128)(2,1)}), bf16[512,2432]{1,0:T(8,128)(2,1)}) %all-gather.2.cloned.1.call-update) | async-done | bytes 2490384 | tf_op jit(solution)/shard_map/all_gather | solution.py:138
  167.8 8.8 %fusion.20 = f32[512,2432]{1,0:T(8,128)} fusion(bf16[608,2432]{1,0:T(8,128)(2,1)S(1)} %copy-done, bf16[512,2432]{1,0:T(8,128)(2,1)} %all-gather.2.cloned.1.call-done, bf16[2432,608]{0,1:T(8,128)(2,1)} %param.25), kind=kOutput, calls=%fused_computation.29 | convolution fusion | flops 3031089152 | bytes 13385728 | tf_op jit(solution)/shard_map/dot_general | solution.py:145
  176.6 109.0 %reduce-scatter.2.cloned.1.call-done = f32[32,2432]{1,0:T(8,128)} async-done(((f32[512,2432]{1,0:T(8,128)}), f32[32,2432]{1,0:T(8,128)}) %reduce-scatter.2.cloned.1.call-update) | async-done | bytes 311312 | tf_op jit(solution)/shard_map/reduce_scatter | solution.py:144
  287.0 1.3 fusion.27
  288.3 1.9 collective-permute-start
  (83 shorter events, 24.8 us)
Async XLA Ops:
  7.2 160.6 %copy-start = (bf16[608,2432]{1,0:T(8,128)(2,1)S(1)}, bf16[608,2432]{1,0:T(8,128)(2,1)}, u32[]{:S(2)}) copy-start(bf16[608,2432]{1,0:T(8,128)(2,1)} %param.26) | copy-start | bytes 8871940
  14.7 12.3 %copy-start.2 = (bf16[1,32,2432]{2,1,0:T(8,128)(2,1)S(1)}, bf16[1,32,2432]{2,1,0:T(8,128)(2,1)}, u32[]{:S(2)}) copy-start(bf16[1,32,2432]{2,1,0:T(8,128)(2,1)} %param.19) | copy-start | bytes 466948
  16.6 29.0 %all-to-all-start = ((bf16[32,16,256]{2,0,1:T(8,128)(2,1)}), bf16[32,16,256]{2,0,1:T(8,128)(2,1)}, u32[]{:S(2)}, u32[]{:S(2)}) async-start(bf16[32,16,256]{2,0,1:T(8,128)(2,1)} %copy.68), calls=%async_computation | async-start | bytes 524288 | tf_op jit(solution)/shard_map/all_to_all | solution.py:73
  45.6 14.9 %all-to-all-start.2 = ((bf16[36,16,256]{2,0,1:T(8,128)(2,1)}), bf16[36,16,256]{2,0,1:T(8,128)(2,1)}, u32[]{:S(2)}, u32[]{:S(2)}) async-start(bf16[36,16,256]{2,0,1:T(8,128)(2,1)} %copy.80), calls=%async_computation.2 | async-start | bytes 655360 | tf_op jit(solution)/shard_map/all_to_all | solution.py:75
  60.5 13.7 %all-to-all-start.1 = ((bf16[36,16,256]{2,0,1:T(8,128)(2,1)}), bf16[36,16,256]{2,0,1:T(8,128)(2,1)S(1)}, u32[]{:S(2)}, u32[]{:S(2)}) async-start(bf16[36,16,256]{2,0,1:T(8,128)(2,1)} %copy.75), calls=%async_computation.1 | async-start | bytes 655360 | tf_op jit(solution)/shard_map/all_to_all | solution.py:74
  74.2 2.2 copy-start.1
  77.2 7.7 %copy-start.6 = (s32[16,4]{1,0:T(8,128)S(1)}, s32[16,4]{1,0:T(8,128)}, u32[]{:S(2)}) copy-start(s32[16,4]{1,0:T(8,128)} %get-tuple-element.13) | copy-start | bytes 772
  77.2 8.4 %copy-start.3 = (f32[1,6,2432]{2,0,1:T(1,128)S(1)}, f32[1,6,2432]{2,0,1:T(1,128)}, u32[]{:S(2)}) copy-start(f32[1,6,2432]{2,0,1:T(1,128)} %param.23) | copy-start | bytes 175108
  79.1 13.2 %all-to-all-start.3 = ((bf16[32,16,256]{2,0,1:T(8,128)(2,1)}), bf16[32,16,256]{2,0,1:T(8,128)(2,1)}, u32[]{:S(2)}, u32[]{:S(2)}) async-start(bf16[32,16,256]{2,0,1:T(8,128)(2,1)} %reshape.355), calls=%async_computation.3 | async-start | bytes 524288 | tf_op jit(solution)/shard_map/all_to_all | solution.py:118
  84.9 82.9 %all-gather.2.cloned.1.call-start = ((), (), s32[]{:S(2)}) async-start(), calls=%async_computation.5 | async-start | bytes 2646016 | tf_op jit(solution)/shard_map/all_gather | solution.py:138
  96.6 6.6 %copy-start.4 = (f32[2432]{0:T(1024)S(1)}, f32[2432]{0:T(1024)}, u32[]{:S(2)}) copy-start(f32[2432]{0:T(1024)} %get-tuple-element.4) | copy-start | bytes 29188
  96.6 6.6 %copy-start.5 = (f32[2432]{0:T(1024)S(1)}, f32[2432]{0:T(1024)}, u32[]{:S(2)}) copy-start(f32[2432]{0:T(1024)} %get-tuple-element.5) | copy-start | bytes 29188
  104.0 181.6 %reduce-scatter.2.cloned.1.call-start = ((), (), s32[]{:S(2)}) async-start(), calls=%async_computation.6 | async-start | bytes 5292032 | tf_op jit(solution)/shard_map/reduce_scatter | solution.py:144
  176.6 110.4 %copy-start.8 = (f32[2432]{0:T(1024)S(1)}, f32[2432]{0:T(1024)}, u32[]{:S(2)}) copy-start(f32[2432]{0:T(1024)} %get-tuple-element.3) | copy-start | bytes 29188
  176.6 110.4 %copy-start.9 = (f32[2432]{0:T(1024)S(1)}, f32[2432]{0:T(1024)}, u32[]{:S(2)}) copy-start(f32[2432]{0:T(1024)} %get-tuple-element.8) | copy-start | bytes 29188
  176.6 114.9 %copy-start.7 = (f32[32,32]{1,0:T(8,128)S(1)}, f32[32,32]{1,0:T(8,128)}, u32[]{:S(2)}) copy-start(f32[32,32]{1,0:T(8,128)} %param.28) | copy-start | bytes 12292
  288.3 3.3 %collective-permute-start = (f32[32,64]{1,0:T(8,128)S(1)}, f32[32,64]{1,0:T(8,128)S(1)}, u32[]{:S(2)}, u32[]{:S(2)}) collective-permute-start(f32[32,64]{1,0:T(8,128)S(1)} %fusion.27), channel_id=1, source_target_pairs={{0,16},{16,0},{1,17},{17,1},{2,18},{18,2},{3,19},{19,3},{4,20},{20... | collective-permute-start | bytes 24584 | tf_op jit(solution)/shard_map/ppermute | solution.py:18
Sparse Core Ops, SparseCore 0:
  104.2 63.5 all-gather.1
  176.8 108.7 reduce-scatter.1
where the time goes:
time: 301 us; the launch traced here: 299 us
  waiting for transfers between devices  184 us (61%)
  local copies, waits for them, and re-layouts  39.3 us (13%)
  starting transfers between devices  27.3 us (9%)
  matrix products  20.8 us (7%)
  between operations  16.5 us (5%)
  other arithmetic  11.7 us (4%)
    reduce_scatter x1, waiting for transfers between devices, body(): lax.psum_scatter(jnp.dot(hidden_all, w_down, preferred_element_type=jnp.f...  109 us
    all_gather x1, waiting for transfers between devices, body(): lax.all_gather(normed, 'seq', axis=0, tiled=True)  63.5 us
    dot_general x1, matrix products, body(): jnp.dot(hidden_all, w_down, preferred_element_type=jnp.float32)  8.82 us
    all_to_all x1, starting transfers between devices, body(): lax.all_to_all(spread(queries[0]), 'seq', split_axis=1, concat_axis=1, ti...  7.47 us
    gather x5, local copies, waits for them, and re-layouts, spread(): jnp.take(rows.reshape(count, HEADS, HEAD_DIM), head_pick, axis=1)  6.69 us
    all_to_all x1, starting transfers between devices, body(): lax.all_to_all(spread(value_rows), 'seq', split_axis=1, concat_axis=1, ti...  6.34 us
    dot_general x1, matrix products, body(): projected = jnp.dot(attended, w_out, preferred_element_type=jnp.float32)  6.33 us
  transfers between devices with their start and end apart: 7, of which 5 were waited for; matrix products, arithmetic and copies ran while one was open for 11% of the time, Pallas kernels for 0%

commit v1 on v0

--- a/solution.py
+++ b/solution.py
@@ -1,6 +1,10 @@
+import functools
+
 import jax
 import jax.numpy as jnp
 from jax import lax
+from jax.experimental import pallas as pl
+from jax.experimental.pallas import tpu as pltpu
 from jax.sharding import PartitionSpec as P
 
 HEADS = 38
@@ -26,6 +30,196 @@
 def sigma_at(index):
     frac = 1.0 - index.astype(jnp.float32) / STEPS
     return shift_value * frac / (1.0 + (shift_value - 1.0) * frac)
+
+
+def ffn_kernel(
+    ca, norm_ref, up_ref, down_ref, out_ref, wu, wd, g, pf, pb, ry0, ry1, rx0, rx1, rxa, ryb, rz, s0, s1, s2,
+    wsem, ssem, gsem, dsem, esem
+):
+    me = lax.axis_index("seq")
+    mz = me // 4
+    mx = lax.rem(me, 2)
+    my = lax.rem(me // 2, 2)
+    xn = mz * 4 + my * 2 + (1 - mx)
+    yn = mz * 4 + (1 - my) * 2 + mx
+    zs = [lax.rem(mz + k, 4) for k in range(4)]
+    zn = [z * 4 + my * 2 + mx for z in zs]
+    width = norm_ref.shape[1]
+    cols = (pl.ds(0, ca), pl.ds(ca, width - ca))
+    a, b = cols
+    load_up = pltpu.make_async_copy(up_ref, wu, wsem.at[0])
+    load_down = pltpu.make_async_copy(down_ref, wd, wsem.at[1])
+    load_up.start()
+    load_down.start()
+    barrier = pltpu.get_barrier_semaphore()
+    peers = (xn, yn, zn[1], zn[2], zn[3])
+    for peer in peers:
+        pl.semaphore_signal(barrier, inc=1, device_id={"seq": peer}, device_id_type=pl.DeviceIdType.MESH)
+    sent = []
+
+    def send(src, dst, recv, peer):
+        copy = pltpu.make_async_remote_copy(
+            src_ref=src, dst_ref=dst, send_sem=ssem.at[len(sent)], recv_sem=recv,
+            device_id={"seq": peer}, device_id_type=pl.DeviceIdType.MESH,
+        )
+        copy.start()
+        sent.append(copy)
+
+    def arrived(dst, recv):
+        pltpu.make_async_remote_copy(
+            src_ref=dst, dst_ref=dst, send_sem=ssem.at[0], recv_sem=recv,
+            device_id={"seq": xn}, device_id_type=pl.DeviceIdType.MESH,
+        ).wait_recv()
+
+    g[0, mz] = norm_ref[...]
+    pl.semaphore_wait(barrier, len(peers))
+    for k in (2, 1, 3):
+        send(norm_ref, g.at[0, mz], gsem.at[0, mz], zn[k])
+    send(norm_ref, g.at[1, mz], gsem.at[1, mz], xn)
+    send(norm_ref, g.at[2, mz], gsem.at[2, mz], yn)
+    for k in (1, 3, 2):
+        z = zs[k]
+        arrived(g.at[0, z], gsem.at[0, z])
+        send(g.at[0, z], g.at[1, z], gsem.at[1, z], xn)
+        send(g.at[0, z], g.at[2, z], gsem.at[2, z], yn)
+
+    def up(q):
+        rows = g[q].reshape(128, width)
+        wide = jnp.dot(rows, wu[...], preferred_element_type=jnp.float32)
+        return jax.nn.gelu(wide, approximate=True).astype(jnp.bfloat16)
+
+    def down(hid, half):
+        made = jnp.dot(hid, wd[:, cols[half]], preferred_element_type=jnp.float32)
+        return made.reshape(4, 32, made.shape[1])
+
+    load_up.wait()
+    for k in (0, 1):
+        z = zs[k]
+        arrived(g.at[1, z], gsem.at[1, z])
+        send(g.at[1, z, :, a], g.at[3, z, :, a], gsem.at[3, z], yn)
+        arrived(g.at[2, z], gsem.at[2, z])
+        send(g.at[2, z, :, b], g.at[3, z, :, b], gsem.at[4, z], xn)
+    hid0 = up(0)
+    for k in (3, 2):
+        z = zs[k]
+        arrived(g.at[1, z], gsem.at[1, z])
+        send(g.at[1, z, :, a], g.at[3, z, :, a], gsem.at[3, z], yn)
+        arrived(g.at[2, z], gsem.at[2, z])
+        send(g.at[2, z, :, b], g.at[3, z, :, b], gsem.at[4, z], xn)
+    load_down.wait()
+    hid1 = up(1)
+    pb[1, :, :, b] = down(hid1, 1).astype(jnp.bfloat16)
+    send(pb.at[1, :, :, b], rx0, dsem.at[0], xn)
+    hid2 = up(2)
+    pb[2, :, :, a] = down(hid2, 0).astype(jnp.bfloat16)
+    send(pb.at[2, :, :, a], ry0, dsem.at[1], yn)
+    pf[1, :, :, a] = down(hid1, 0)
+    pf[2, :, :, b] = down(hid2, 1)
+    pf[0, :, :, a] = down(hid0, 0)
+    pf[0, :, :, b] = down(hid0, 1)
+    for z in zs:
+        arrived(g.at[3, z, :, a], gsem.at[3, z])
+        arrived(g.at[3, z, :, b], gsem.at[4, z])
+    hid3 = up(3)
+    order = (2, 1, 3, 0)
+    pb[3, :, :, a] = down(hid3, 0).astype(jnp.bfloat16)
+    for k in order:
+        send(pb.at[3, zs[k], :, a], ry1.at[zs[k]], esem.at[0, zs[k]], yn)
+    pb[3, :, :, b] = down(hid3, 1).astype(jnp.bfloat16)
+    for k in order:
+        send(pb.at[3, zs[k], :, b], rx1.at[zs[k]], esem.at[1, zs[k]], xn)
+    for k in order:
+        z = zs[k]
+        arrived(ry1.at[z], esem.at[0, z])
+        s1[z] = (pf[1, z, :, a] + ry1[z].astype(jnp.float32)).astype(jnp.bfloat16)
+        send(s1.at[z], rxa.at[z], esem.at[2, z], xn)
+        arrived(rx1.at[z], esem.at[1, z])
+        s2[z] = (pf[2, z, :, b] + rx1[z].astype(jnp.float32)).astype(jnp.bfloat16)
+        send(s2.at[z], ryb.at[z], esem.at[3, z], yn)
+    arrived(rx0, dsem.at[0])
+    arrived(ry0, dsem.at[1])
+    for k in order:
+        z = zs[k]
+        arrived(rxa.at[z], esem.at[2, z])
+        arrived(ryb.at[z], esem.at[3, z])
+        sum_a = pf[0, z, :, a] + ry0[z].astype(jnp.float32) + rxa[z].astype(jnp.float32)
+        sum_b = pf[0, z, :, b] + rx0[z].astype(jnp.float32) + ryb[z].astype(jnp.float32)
+        if k:
+            s0[z, :, a] = sum_a.astype(jnp.bfloat16)
+            s0[z, :, b] = sum_b.astype(jnp.bfloat16)
+            send(s0.at[z], rz.at[mz], esem.at[4, mz], zn[k])
+        else:
+            out_ref[:, a] = sum_a
+            out_ref[:, b] = sum_b
+    for k in (1, 3, 2):
+        arrived(rz.at[zs[k]], esem.at[4, zs[k]])
+        out_ref[...] += rz[zs[k]].astype(jnp.float32)
+    for copy in sent:
+        copy.wait_send()
+
+
+def ffn_16(normed, w_up, w_down):
+    rows, width = normed.shape
+    hidden = w_up.shape[1]
+    ca = (width // 128 + 1) // 2 * 128
+    cb = width - ca
+    half = jnp.bfloat16
+    return pl.pallas_call(
+        functools.partial(ffn_kernel, ca),
+        out_shape=jax.ShapeDtypeStruct((rows, width), jnp.float32),
+        in_specs=[
+            pl.BlockSpec(memory_space=pltpu.VMEM),
+            pl.BlockSpec(memory_space=pl.ANY),
+            pl.BlockSpec(memory_space=pl.ANY),
+        ],
+        out_specs=pl.BlockSpec(memory_space=pltpu.VMEM),
+        scratch_shapes=[
+            pltpu.VMEM((width, hidden), half),
+            pltpu.VMEM((hidden, width), half),
+            pltpu.VMEM((4, 4, rows, width), half),
+            pltpu.VMEM((3, 4, rows, width), jnp.float32),
+            pltpu.VMEM((4, 4, rows, width), half),
+            pltpu.VMEM((4, rows, ca), half),
+            pltpu.VMEM((4, rows, ca), half),
+            pltpu.VMEM((4, rows, cb), half),
+            pltpu.VMEM((4, rows, cb), half),
+            pltpu.VMEM((4, rows, ca), half),
+            pltpu.VMEM((4, rows, cb), half),
+            pltpu.VMEM((4, rows, width), half),
+            pltpu.VMEM((4, rows, width), half),
+            pltpu.VMEM((4, rows, ca), half),
+            pltpu.VMEM((4, rows, cb), half),
+            pltpu.SemaphoreType.DMA((2,)),
+            pltpu.SemaphoreType.DMA((48,)),
+            pltpu.SemaphoreType.DMA((5, 4)),
+            pltpu.SemaphoreType.DMA((2,)),
+            pltpu.SemaphoreType.DMA((5, 4)),
+        ],
+        cost_estimate=pl.CostEstimate(
+            flops=4 * 16 * rows * width * hidden, bytes_accessed=4 * width * hidden, transcendentals=16 * rows * hidden
+        ),
+        compiler_params=pltpu.CompilerParams(
+            collective_id=0, has_side_effects=True, vmem_limit_bytes=44 * 2**20
+        ),
+    )(normed, w_up, w_down)
+
+
+def ffn_any(normed, w_up, w_down):
+    hidden_all = jax.nn.gelu(
+        jnp.dot(
+            lax.all_gather(normed, "seq", axis=0, tiled=True),
+            w_up,
+            preferred_element_type=jnp.float32,
+        ),
+        approximate=True,
+    ).astype(jnp.bfloat16)
+    mlp_out = lax.psum_scatter(
+        jnp.dot(hidden_all, w_down, preferred_element_type=jnp.float32),
+        "seq",
+        scatter_dimension=0,
+        tiled=True,
+    )
+    return mlp_out
 
 
 def body(
@@ -61,13 +255,15 @@
     targets = jnp.arange(seq_count, dtype=jnp.int32)
     first_head = targets * unit_count // img_all
     slot_heads = first_head[:, None] + jnp.arange(head_span, dtype=jnp.int32)[None, :]
-    head_pick = jnp.minimum(slot_heads, HEADS - 1).reshape(-1)
 
     def spread(rows):
-        count = rows.shape[0]
-        return jnp.take(rows.reshape(count, HEADS, HEAD_DIM), head_pick, axis=1).reshape(
-            count, seq_count, slot_width
-        )
+        parts = []
+        for target in range(seq_count):
+            lead_head = target * unit_count // img_all
+            for slot in range(lead_head, lead_head + head_span):
+                head = min(slot, HEADS - 1)
+                parts.append(rows[:, head * HEAD_DIM : (head + 1) * HEAD_DIM])
+        return jnp.concatenate(parts, 1).reshape(rows.shape[0], seq_count, slot_width)
 
     query_in, key_in, value_in = (
         lax.all_to_all(spread(queries[0]), "seq", split_axis=1, concat_axis=1, tiled=True),
@@ -133,20 +329,10 @@
     projected = jnp.dot(attended, w_out, preferred_element_type=jnp.float32)
     middle = hidden_in[0].astype(jnp.float32) + mods[0] * projected
     normed = (layer_norm(middle) * (1.0 + mods[2]) + mods[1]).astype(jnp.bfloat16)
-    hidden_all = jax.nn.gelu(
-        jnp.dot(
-            lax.all_gather(normed, "seq", axis=0, tiled=True),
-            w_up,
-            preferred_element_type=jnp.float32,
-        ),
-        approximate=True,
-    ).astype(jnp.bfloat16)
-    mlp_out = lax.psum_scatter(
-        jnp.dot(hidden_all, w_down, preferred_element_type=jnp.float32),
-        "seq",
-        scatter_dimension=0,
-        tiled=True,
-    )
+    if seq_count == 16 and img_rows == 32:
+        mlp_out = ffn_16(normed, w_up, w_down)
+    else:
+        mlp_out = ffn_any(normed, w_up, w_down)
     final = middle + mods[3] * mlp_out
     head_in = (layer_norm(final) * (1.0 + mods[5]) + mods[4]).astype(jnp.bfloat16)
     own_velocity = jnp.dot(head_in, w_final, preferred_element_type=jnp.float32)

time: 301 us -> 142 us (0.47)
  waiting for transfers between devices: 184 us -> 19.4 us
  Pallas kernels: 0 us -> 60.2 us
  local copies, waits for them, and re-layouts: 39.3 us -> 16.7 us
  between operations: 16.5 us -> 3.07 us
  matrix products: 20.8 us -> 10.3 us
  other arithmetic: 11.7 us -> 6.14 us
    reduce_scatter x1 -> x0, waiting for transfers between devices: 109 us -> none  [body(): lax.psum_scatter(jnp.dot(hidden_all, w_down, preferred_element_type=jnp.f...]
    all_gather x1 -> x0, waiting for transfers between devices: 63.5 us -> none  [body(): lax.all_gather(normed, 'seq', axis=0, tiled=True)]
    pallas_call x0 -> x1, Pallas kernels: none -> 60.2 us  [ffn_16(): pl.pallas_call(functools.partial(ffn_kernel, ca), out_shape=jax.ShapeDtyp...]
    dot_general x1 -> x0, matrix products: 8.82 us -> none  [body(): jnp.dot(hidden_all, w_down, preferred_element_type=jnp.float32)]
    all_to_all x1, waiting for transfers between devices: 0.83 us -> 7.65 us  [body(): lax.all_to_all(spread(key_rows), 'seq', split_axis=1, concat_axis=1, tile...]
    gather x5 -> x0, local copies, waits for them, and re-layouts: 6.69 us -> none  [spread(): jnp.take(rows.reshape(count, HEADS, HEAD_DIM), head_pick, axis=1)]
    concatenate x8 -> x3, local copies, waits for them, and re-layouts: 4.62 us -> 0.28 us  [spread(): jnp.concatenate(parts, 1).reshape(rows.shape[0], seq_count, slot_width)]
    unnamed x20 -> x21, local copies, waits for them, and re-layouts: 0.05 us -> 4.36 us
  transfers between devices with their start and end apart: 7 -> 5, of which waited for: 5 -> 4; matrix products, arithmetic and copies ran while one was open for 11% -> 8% of each run, Pallas kernels for 0% -> 0%
where the time goes in v1:
time: 142 us; the launch traced here: 141 us
  Pallas kernels  60.2 us (42%)
  starting transfers between devices  25.2 us (18%)
  waiting for transfers between devices  19.4 us (14%)
  local copies, waits for them, and re-layouts  16.7 us (12%)
  matrix products  10.3 us (7%)
  other arithmetic  6.14 us (4%)
  between operations  3.07 us (2%)
    pallas_call x1, Pallas kernels, ffn_16(): pl.pallas_call(functools.partial(ffn_kernel, ca), out_shape=jax.ShapeDtyp...  60.2 us
    all_to_all x1, waiting for transfers between devices, body(): lax.all_to_all(spread(key_rows), 'seq', split_axis=1, concat_axis=1, tile...  7.65 us
    all_to_all x1, waiting for transfers between devices, body(): lax.all_to_all(spread(value_rows), 'seq', split_axis=1, concat_axis=1, ti...  7.56 us
    all_to_all x1, starting transfers between devices, body(): lax.all_to_all(spread(queries[0]), 'seq', split_axis=1, concat_axis=1, ti...  7.41 us
    dot_general x1, matrix products, body(): projected = jnp.dot(attended, w_out, preferred_element_type=jnp.float32)  6.43 us
    all_to_all x1, starting transfers between devices, body(): lax.all_to_all(going, 'seq', split_axis=1, concat_axis=1, tiled=True)  5.81 us
    all_to_all x1, starting transfers between devices, body(): lax.all_to_all(spread(key_rows), 'seq', split_axis=1, concat_axis=1, tile...  5.58 us
    all_to_all x1, starting transfers between devices, body(): lax.all_to_all(spread(value_rows), 'seq', split_axis=1, concat_axis=1, ti...  4.79 us
  transfers between devices with their start and end apart: 5, of which 4 were waited for; matrix products, arithmetic and copies ran while one was open for 8% of the time, Pallas kernels for 0%

profile of v1, /device:TPU:1, one launch (start us, length us, event | category | flops | bytes accessed | tf_op | source)
XLA Modules:
  0.0 141.0 jit_solution(6249862585508333946)
XLA Ops:
  0.7 1.1 fusion.54
  1.8 0.8 slice.470
  2.6 0.8 slice.471
  3.5 0.7 copy.67
  4.2 7.4 %all-to-all-start = ((bf16[32,16,256]{2,0,1:T(8,128)(2,1)}), bf16[32,16,256]{2,0,1:T(8,128)(2,1)S(1)}, u32[]{:S(2)}, u32[]{:S(2)}) async-start(bf16[32,16,256]{2,0,1:T(8,128)(2,1)} %bitcast.58), calls=%async_computation | async-start | bytes 524288 | tf_op jit(solution)/shard_map/all_to_all | solution.py:269
  11.6 1.0 fusion.47
  12.6 1.0 fusion.46
  13.7 0.8 fusion.32
  15.5 0.8 copy.45
  16.9 0.8 copy.47
  17.8 1.8 %all-to-all-done = bf16[32,16,256]{2,0,1:T(8,128)(2,1)S(1)} async-done(((bf16[32,16,256]{2,0,1:T(8,128)(2,1)}), bf16[32,16,256]{2,0,1:T(8,128)(2,1)S(1)}, u32[]{:S(2)}, u32[]{:S(2)}) %all-to-all-start) | async-done | bytes 262176 | tf_op jit(solution)/shard_map/all_to_all | solution.py:269
  19.6 4.8 %all-to-all-start.2 = ((bf16[36,16,256]{2,0,1:T(8,128)(2,1)}), bf16[36,16,256]{2,0,1:T(8,128)(2,1)S(1)}, u32[]{:S(2)}, u32[]{:S(2)}) async-start(bf16[36,16,256]{2,0,1:T(8,128)(2,1)} %copy.47), calls=%async_computation.2 | async-start | bytes 655360 | tf_op jit(solution)/shard_map/all_to_all | solution.py:271
  24.8 0.3 copy.43
  25.2 7.6 %all-to-all-done.2 = bf16[36,16,256]{2,0,1:T(8,128)(2,1)S(1)} async-done(((bf16[36,16,256]{2,0,1:T(8,128)(2,1)}), bf16[36,16,256]{2,0,1:T(8,128)(2,1)S(1)}, u32[]{:S(2)}, u32[]{:S(2)}) %all-to-all-start.2) | async-done | bytes 294944 | tf_op jit(solution)/shard_map/all_to_all | solution.py:271
  32.7 5.6 %all-to-all-start.1 = ((bf16[36,16,256]{2,0,1:T(8,128)(2,1)}), bf16[36,16,256]{2,0,1:T(8,128)(2,1)S(1)}, u32[]{:S(2)}, u32[]{:S(2)}) async-start(bf16[36,16,256]{2,0,1:T(8,128)(2,1)} %copy.45), calls=%async_computation.1 | async-start | bytes 655360 | tf_op jit(solution)/shard_map/all_to_all | solution.py:270
  38.9 7.6 %all-to-all-done.1 = bf16[36,16,256]{2,0,1:T(8,128)(2,1)S(1)} async-done(((bf16[36,16,256]{2,0,1:T(8,128)(2,1)}), bf16[36,16,256]{2,0,1:T(8,128)(2,1)S(1)}, u32[]{:S(2)}, u32[]{:S(2)}) %all-to-all-start.1) | async-done | bytes 294944 | tf_op jit(solution)/shard_map/all_to_all | solution.py:270
  46.6 0.6 fusion.55
  47.1 0.4 fusion.2
  47.6 0.8 fusion.7
  48.7 0.4 copy.57
  49.2 1.0 reshape.263
  50.2 5.8 %all-to-all-start.3 = ((bf16[32,16,256]{2,0,1:T(8,128)(2,1)}), bf16[32,16,256]{2,0,1:T(8,128)(2,1)}, u32[]{:S(2)}, u32[]{:S(2)}) async-start(bf16[32,16,256]{2,0,1:T(8,128)(2,1)} %reshape.263), calls=%async_computation.3 | async-start | bytes 524288 | tf_op jit(solution)/shard_map/all_to_all | solution.py:314
  56.0 4.2 %copy.55.up_ref = bf16[2432,608]{1,0:T(8,128)(2,1)S(1)} copy(bf16[2432,608]{0,1:T(8,128)(2,1)} %param.23) | data formatting | bytes 5914624 | tf_op args[8]
  60.3 0.8 add_reduce_fusion
  61.0 2.4 %all-to-all-done.3 = bf16[32,16,256]{2,0,1:T(8,128)(2,1)} async-done(((bf16[32,16,256]{2,0,1:T(8,128)(2,1)}), bf16[32,16,256]{2,0,1:T(8,128)(2,1)}, u32[]{:S(2)}, u32[]{:S(2)}) %all-to-all-start.3) | async-done | bytes 262176 | tf_op jit(solution)/shard_map/all_to_all | solution.py:314
  63.4 2.0 %reshape.264 = bf16[32,16,4,64]{3,2,0,1:T(4,128)(2,1)} reshape(bf16[32,16,256]{2,0,1:T(8,128)(2,1)} %all-to-all-done.3) | data formatting | bytes 524288 | tf_op jit(solution)/shard_map/reshape | solution.py:321
  65.4 2.2 %fusion.11 = bf16[32,38,64]{2,1,0:T(8,128)(2,1)} fusion(bf16[32,16,4,64]{3,2,0,1:T(4,128)(2,1)} %reshape.264, s32[16,4]{0,1:T(4,128)S(1)} %iota_add_fusion.1), kind=kOutput, calls=%fused_computation.13 | convolution fusion | flops 10041728 | bytes 418048 | tf_op jit(solution)/shard_map/rjsd,jsh->rhd/dot_general | solution.py:319
  67.7 1.9 %convert_element_type.42 = bf16[32,2432]{1,0:T(8,128)(2,1)} reshape(bf16[32,38,64]{2,1,0:T(8,128)(2,1)} %fusion.11) | data formatting | bytes 311296 | tf_op jit(solution)/shard_map/convert_element_type | solution.py:326
  69.6 6.4 %fusion.56 = (f32[32]{0:T(128)S(1)}, f32[32,2432]{1,0:T(8,128)S(1)}) fusion(bf16[32,2432]{1,0:T(8,128)(2,1)} %convert_element_type.42, bf16[2432,2432]{1,0:T(8,128)(2,1)} %param.22, f32[2432]{0:T(1024)S(1)} %get-tuple-element.6, bf16[1,32,2432]{2,1,0:T(8,128)(2,1)} %param.20), kind=kOutput, calls=%fused_computation.161 | convolution fusion | flops 378847200 | bytes 12461696 | tf_op jit(solution)/shard_map/dot_general | solution.py:329
  76.4 60.2 %shard_map.158 = f32[32,2432]{1,0:T(8,128)S(1)} custom-call(bf16[32,2432]{1,0:T(8,128)(2,1)S(1)} %add_convert_fusion.1.norm_ref, bf16[2432,608]{1,0:T(8,128)(2,1)S(1)} %copy.55.up_ref, bf16[608,2432]{1,0:T(8,128)(2,1)S(1)} %copy-done.1), custom_call_target="tpu_custom_call" | custom-call | flops 3028287488 | bytes 5914624 | tf_op jit(solution)/shard_map/pallas_call | solution.py:167
  137.3 1.6 %collective-permute-start = (f32[32,64]{1,0:T(8,128)S(1)}, f32[32,64]{1,0:T(8,128)S(1)}, u32[]{:S(2)}, u32[]{:S(2)}) collective-permute-start(f32[32,64]{1,0:T(8,128)S(1)} %fusion.13), channel_id=1, source_target_pairs={{0,16},{16,0},{1,17},{17,1},{2,18},{18,2},{3,19},{19,3},{4,20},{20... | collective-permute-start | bytes 24584 | tf_op jit(solution)/shard_map/ppermute | solution.py:22
  140.3 0.7 multiply_add_fusion.1
  (60 shorter events, 3.5 us)
Async XLA Ops:
  0.6 136.4 %copy-start = (bf16[2432,64]{0,1:T(8,128)(2,1)S(1)}, bf16[2432,64]{0,1:T(8,128)(2,1)}, u32[]{:S(2)}) copy-start(bf16[2432,64]{0,1:T(8,128)(2,1)} %param.25) | copy-start | bytes 933892
  0.6 14.6 %copy-start.2 = (bf16[1,32,2432]{2,1,0:T(8,128)(2,1)S(1)}, bf16[1,32,2432]{2,1,0:T(8,128)(2,1)}, u32[]{:S(2)}) copy-start(bf16[1,32,2432]{2,1,0:T(8,128)(2,1)} %param.16) | copy-start | bytes 466948
  0.7 14.6 %copy-start.4 = (bf16[1,4,2432]{2,1,0:T(4,128)(2,1)S(1)}, bf16[1,4,2432]{2,1,0:T(4,128)(2,1)}, u32[]{:S(2)}) copy-start(bf16[1,4,2432]{2,1,0:T(4,128)(2,1)} %param.18) | copy-start | bytes 58372
  0.7 15.7 %copy-start.3 = (bf16[1,32,2432]{2,1,0:T(8,128)(2,1)S(1)}, bf16[1,32,2432]{2,1,0:T(8,128)(2,1)}, u32[]{:S(2)}) copy-start(bf16[1,32,2432]{2,1,0:T(8,128)(2,1)} %param.17) | copy-start | bytes 466948
  0.7 15.7 %copy-start.5 = (bf16[1,4,2432]{2,1,0:T(4,128)(2,1)S(1)}, bf16[1,4,2432]{2,1,0:T(4,128)(2,1)}, u32[]{:S(2)}) copy-start(bf16[1,4,2432]{2,1,0:T(4,128)(2,1)} %param.19) | copy-start | bytes 58372
  4.2 15.4 %all-to-all-start = ((bf16[32,16,256]{2,0,1:T(8,128)(2,1)}), bf16[32,16,256]{2,0,1:T(8,128)(2,1)S(1)}, u32[]{:S(2)}, u32[]{:S(2)}) async-start(bf16[32,16,256]{2,0,1:T(8,128)(2,1)} %bitcast.58), calls=%async_computation | async-start | bytes 524288 | tf_op jit(solution)/shard_map/all_to_all | solution.py:269
  19.6 13.2 %all-to-all-start.2 = ((bf16[36,16,256]{2,0,1:T(8,128)(2,1)}), bf16[36,16,256]{2,0,1:T(8,128)(2,1)S(1)}, u32[]{:S(2)}, u32[]{:S(2)}) async-start(bf16[36,16,256]{2,0,1:T(8,128)(2,1)} %copy.47), calls=%async_computation.2 | async-start | bytes 655360 | tf_op jit(solution)/shard_map/all_to_all | solution.py:271
  32.7 13.8 %all-to-all-start.1 = ((bf16[36,16,256]{2,0,1:T(8,128)(2,1)}), bf16[36,16,256]{2,0,1:T(8,128)(2,1)S(1)}, u32[]{:S(2)}, u32[]{:S(2)}) async-start(bf16[36,16,256]{2,0,1:T(8,128)(2,1)} %copy.45), calls=%async_computation.1 | async-start | bytes 655360 | tf_op jit(solution)/shard_map/all_to_all | solution.py:270
  50.2 13.2 %all-to-all-start.3 = ((bf16[32,16,256]{2,0,1:T(8,128)(2,1)}), bf16[32,16,256]{2,0,1:T(8,128)(2,1)}, u32[]{:S(2)}, u32[]{:S(2)}) async-start(bf16[32,16,256]{2,0,1:T(8,128)(2,1)} %reshape.263), calls=%async_computation.3 | async-start | bytes 524288 | tf_op jit(solution)/shard_map/all_to_all | solution.py:314
  56.0 4.2 %copy-start.6 = (f32[1,6,2432]{2,0,1:T(1,128)S(1)}, f32[1,6,2432]{2,0,1:T(1,128)}, u32[]{:S(2)}) copy-start(f32[1,6,2432]{2,0,1:T(1,128)} %param.21) | copy-start | bytes 175108
  69.6 6.8 %copy-start.1 = (bf16[608,2432]{1,0:T(8,128)(2,1)S(1)}, bf16[608,2432]{1,0:T(8,128)(2,1)}, u32[]{:S(2)}) copy-start(bf16[608,2432]{1,0:T(8,128)(2,1)} %down_ref.1) | copy-start | bytes 8871940
  76.4 60.6 %copy-start.8 = (f32[2432]{0:T(1024)S(1)}, f32[2432]{0:T(1024)}, u32[]{:S(2)}) copy-start(f32[2432]{0:T(1024)} %get-tuple-element.7) | copy-start | bytes 29188
  76.4 63.9 %copy-start.7 = (f32[32,32]{1,0:T(8,128)S(1)}, f32[32,32]{1,0:T(8,128)}, u32[]{:S(2)}) copy-start(f32[32,32]{1,0:T(8,128)} %param.26) | copy-start | bytes 12292
  137.3 3.0 %collective-permute-start = (f32[32,64]{1,0:T(8,128)S(1)}, f32[32,64]{1,0:T(8,128)S(1)}, u32[]{:S(2)}, u32[]{:S(2)}) collective-permute-start(f32[32,64]{1,0:T(8,128)S(1)} %fusion.13), channel_id=1, source_target_pairs={{0,16},{16,0},{1,17},{17,1},{2,18},{18,2},{3,19},{19,3},{4,20},{20... | collective-permute-start | bytes 24584 | tf_op jit(solution)/shard_map/ppermute | solution.py:22

commit v2 on v1

--- a/solution.py
+++ b/solution.py
@@ -85,7 +85,7 @@
 
     def up(q):
         rows = g[q].reshape(128, width)
-        wide = jnp.dot(rows, wu[...], preferred_element_type=jnp.float32)
+        wide = lax.dot_general(rows, wu[...], (((1,), (1,)), ((), ())), preferred_element_type=jnp.float32)
         return jax.nn.gelu(wide, approximate=True).astype(jnp.bfloat16)
 
     def down(hid, half):
@@ -174,7 +174,7 @@
         ],
         out_specs=pl.BlockSpec(memory_space=pltpu.VMEM),
         scratch_shapes=[
-            pltpu.VMEM((width, hidden), half),
+            pltpu.VMEM((hidden, width), half),
             pltpu.VMEM((hidden, width), half),
             pltpu.VMEM((4, 4, rows, width), half),
             pltpu.VMEM((3, 4, rows, width), jnp.float32),
@@ -201,7 +201,209 @@
         compiler_params=pltpu.CompilerParams(
             collective_id=0, has_side_effects=True, vmem_limit_bytes=44 * 2**20
         ),
-    )(normed, w_up, w_down)
+    )(normed, w_up.T, w_down)
+
+
+EXTRA = (5, 8, 6)
+PAIR = 2 * HEAD_DIM
+
+
+def attend_kernel(
+    rows, st_ref, bias_ref, wo_ref, out_ref, wo, land, kb, vb, res, att, wsem, ssem, xsem, rsem, osem, asem, lsem
+):
+    me = lax.axis_index("seq")
+    mesh_id = pl.DeviceIdType.MESH
+    deep = rows * 3 + 16
+
+    def lanes(pair):
+        return pl.ds(pl.multiple_of(pair * PAIR, PAIR), PAIR)
+
+    def peer_of(k):
+        return lax.rem(me + k, 16)
+
+    def remote(src, dst, sent, got, peer):
+        return pltpu.make_async_remote_copy(
+            src_ref=src, dst_ref=dst, send_sem=sent, recv_sem=got, device_id={"seq": peer}, device_id_type=mesh_id
+        )
+
+    load = pltpu.make_async_copy(wo_ref, wo, wsem.at[0])
+    load.start()
+    own = pltpu.make_async_copy(st_ref.at[:, lanes(me)], land.at[0, me], lsem.at[0])
+    own.start()
+    barrier = pltpu.get_barrier_semaphore()
+
+    def greet(k, c):
+        pl.semaphore_signal(barrier, inc=1, device_id={"seq": peer_of(k)}, device_id_type=mesh_id)
+        return c
+
+    lax.fori_loop(1, 16, greet, 0)
+    pl.semaphore_wait(barrier, 15)
+
+    def extra_in(e, owner):
+        return remote(st_ref.at[:, lanes(16 + e)], land.at[1, me], xsem.at[e], rsem.at[1, me], owner)
+
+    def extra_own(e):
+        return pltpu.make_async_copy(st_ref.at[:, lanes(16 + e)], land.at[1, me], lsem.at[1])
+
+    def pair_in(k):
+        peer = peer_of(k)
+        return remote(st_ref.at[:, lanes(peer)], land.at[0, me], ssem.at[k], rsem.at[0, me], peer)
+
+    def go(k, c):
+        pair_in(k).start()
+        return c
+
+    lax.fori_loop(1, 16, go, 0)
+    for e, owner in enumerate(EXTRA):
+
+        @pl.when(me != owner)
+        def _():
+            extra_in(e, owner).start()
+
+        @pl.when(me == owner)
+        def _():
+            extra_own(e).start()
+
+    def back(u, dst, pair):
+        return remote(res.at[u, dst], att.at[:, lanes(pair)], osem.at[u, dst], asem.at[pair], dst)
+
+    def unit(u, pair, local):
+        def arrive(k, c):
+            src = peer_of(k)
+            remote(land.at[u, src], land.at[u, src], ssem.at[0], rsem.at[u, src], src).wait_recv()
+            return c
+
+        lax.fori_loop(1, 16, arrive, 0)
+        local.wait()
+        text = land[u, :, 3 * rows : deep, :].reshape(256, PAIR)
+        slot = lax.broadcasted_iota(jnp.int32, (64, 256), 0)
+        place = lax.broadcasted_iota(jnp.int32, (64, 256), 1)
+        start = (slot >> 2) * 16 + (slot & 3)
+        for kind, buf in ((0, kb), (1, vb)):
+            pick = jnp.where(place == start + 4 * kind, 1.0, 0.0).astype(jnp.bfloat16)
+            buf[512:576, :] = jnp.dot(pick, text, preferred_element_type=jnp.float32).astype(jnp.bfloat16)
+            buf[0:512, :] = land[u, :, (kind + 1) * rows : (kind + 2) * rows, :].reshape(512, PAIR)
+        low = lax.broadcasted_iota(jnp.int32, (4 * rows, PAIR), 1) < HEAD_DIM
+
+        def chunk(c, carry):
+            q = land[u, pl.ds(c * 4, 4), 0:rows, :].reshape(4 * rows, PAIR)
+            made = []
+            for head in range(2):
+                mine = low if head == 0 else jnp.logical_not(low)
+                q_one = jnp.where(mine, q, jnp.zeros_like(q))
+                scores = lax.dot_general(
+                    q_one, kb[...], (((1,), (1,)), ((), ())), preferred_element_type=jnp.float32
+                ) * (HEAD_DIM ** (-0.5))
+                scores = scores + bias_ref[...]
+                top = jnp.max(scores, -1, keepdims=True)
+                weights = jnp.exp(scores - top)
+                total = jnp.sum(weights, -1, keepdims=True)
+                mixed = jnp.dot(weights.astype(jnp.bfloat16), vb[...], preferred_element_type=jnp.float32)
+                made.append(mixed / total)
+            both = jnp.where(low, made[0], made[1]).astype(jnp.bfloat16)
+            for j in range(4):
+                dst = c * 4 + j
+                res[u, dst] = both[j * rows : (j + 1) * rows, :]
+
+                @pl.when(dst != me)
+                def _():
+                    back(u, dst, pair).start()
+
+                @pl.when(dst == me)
+                def _():
+                    att[:, lanes(pair)] = both[j * rows : (j + 1) * rows, :]
+
+            return carry
+
+        lax.fori_loop(0, 4, chunk, 0)
+
+    unit(0, me, own)
+    for e, owner in enumerate(EXTRA):
+
+        @pl.when(me == owner)
+        def _():
+            unit(1, 16 + e, extra_own(e))
+
+    def home(pair, src):
+        spot = att.at[:, lanes(pair)]
+        remote(spot, spot, ssem.at[0], asem.at[pair], src).wait_recv()
+
+    def collect(k, c):
+        home(peer_of(k), peer_of(k))
+        return c
+
+    lax.fori_loop(1, 16, collect, 0)
+    for e, owner in enumerate(EXTRA):
+
+        @pl.when(me != owner)
+        def _():
+            home(16 + e, owner)
+
+    load.wait()
+    out_ref[...] = jnp.dot(att[...], wo[...], preferred_element_type=jnp.float32)
+
+    def finish(k, c):
+        pair_in(k).wait_send()
+        back(0, peer_of(k), me).wait_send()
+        return c
+
+    lax.fori_loop(1, 16, finish, 0)
+    for e, owner in enumerate(EXTRA):
+
+        @pl.when(me != owner)
+        def _():
+            extra_in(e, owner).wait_send()
+
+        @pl.when(me == owner)
+        def _():
+            def finish_extra(k, c):
+                back(1, peer_of(k), 16 + e).wait_send()
+                return c
+
+            lax.fori_loop(1, 16, finish_extra, 0)
+
+
+def attend_16(queries, image_keys, image_values, text_keys, text_values, w_out, length):
+    rows, width = queries.shape
+    half = jnp.bfloat16
+    stacked = jnp.concatenate(
+        [queries, image_keys, image_values, text_keys, text_values, jnp.zeros((8, width), half)], 0
+    )
+    deep = stacked.shape[0]
+    key = jnp.arange(576, dtype=jnp.int32)
+    bias = jnp.where(key - 512 < length, 0.0, -1e30).astype(jnp.float32)[None, :]
+    pairs = width // PAIR
+    return pl.pallas_call(
+        functools.partial(attend_kernel, rows),
+        out_shape=jax.ShapeDtypeStruct((rows, width), jnp.float32),
+        in_specs=[
+            pl.BlockSpec(memory_space=pltpu.VMEM),
+            pl.BlockSpec(memory_space=pltpu.VMEM),
+            pl.BlockSpec(memory_space=pl.ANY),
+        ],
+        out_specs=pl.BlockSpec(memory_space=pltpu.VMEM),
+        scratch_shapes=[
+            pltpu.VMEM((width, width), half),
+            pltpu.VMEM((2, 16, deep, PAIR), half),
+            pltpu.VMEM((576, PAIR), half),
+            pltpu.VMEM((576, PAIR), half),
+            pltpu.VMEM((2, 16, rows, PAIR), half),
+            pltpu.VMEM((rows, width), half),
+            pltpu.SemaphoreType.DMA((1,)),
+            pltpu.SemaphoreType.DMA((16,)),
+            pltpu.SemaphoreType.DMA((len(EXTRA),)),
+            pltpu.SemaphoreType.DMA((2, 16)),
+            pltpu.SemaphoreType.DMA((2, 16)),
+            pltpu.SemaphoreType.DMA((pairs,)),
+            pltpu.SemaphoreType.DMA((2,)),
+        ],
+        cost_estimate=pl.CostEstimate(
+            flops=2 * rows * width * width, bytes_accessed=2 * width * width, transcendentals=2 * 512 * 576
+        ),
+        compiler_params=pltpu.CompilerParams(
+            collective_id=1, has_side_effects=True, vmem_limit_bytes=44 * 2**20
+        ),
+    )(stacked, bias, w_out)
 
 
 def ffn_any(normed, w_up, w_down):
@@ -220,6 +422,94 @@
         tiled=True,
     )
     return mlp_out
+
+
+def attend_any(queries, image_keys, image_values, text_keys, text_values, w_out, length):
+    img_rows, width = queries.shape[1:]
+    text_rows = text_keys.shape[1]
+    both_rows = img_rows + text_rows
+    score_scale = HEAD_DIM ** (-0.5)
+    key_rows = jnp.concatenate([image_keys[0], text_keys[0]], 0)
+    value_rows = jnp.concatenate([image_values[0], text_values[0]], 0)
+    seq_count = lax.axis_size("seq")
+    img_all = img_rows * seq_count
+    unit_count = HEADS * img_rows
+    head_span = min(HEADS, (unit_count - 1) // img_all + 2)
+    slot_width = head_span * HEAD_DIM
+    targets = jnp.arange(seq_count, dtype=jnp.int32)
+    first_head = targets * unit_count // img_all
+    slot_heads = first_head[:, None] + jnp.arange(head_span, dtype=jnp.int32)[None, :]
+
+    def spread(rows):
+        parts = []
+        for target in range(seq_count):
+            lead_head = target * unit_count // img_all
+            for slot in range(lead_head, lead_head + head_span):
+                head = min(slot, HEADS - 1)
+                parts.append(rows[:, head * HEAD_DIM : (head + 1) * HEAD_DIM])
+        return jnp.concatenate(parts, 1).reshape(rows.shape[0], seq_count, slot_width)
+
+    query_in, key_in, value_in = (
+        lax.all_to_all(spread(queries[0]), "seq", split_axis=1, concat_axis=1, tiled=True),
+        lax.all_to_all(spread(key_rows), "seq", split_axis=1, concat_axis=1, tiled=True),
+        lax.all_to_all(spread(value_rows), "seq", split_axis=1, concat_axis=1, tiled=True),
+    )
+    myself = lax.axis_index("seq")
+    lead = myself * unit_count // img_all
+    offset = myself * unit_count - lead * img_all
+    query_flat = (
+        query_in.reshape(img_rows, seq_count, head_span, HEAD_DIM)
+        .transpose(2, 1, 0, 3)
+        .reshape(head_span * img_all, HEAD_DIM)
+    )
+    query_units = lax.dynamic_slice_in_dim(query_flat, offset, unit_count, 0)
+    unit_slot = (offset + jnp.arange(unit_count, dtype=jnp.int32)) // img_all
+    slot_match = unit_slot[:, None] == jnp.arange(head_span, dtype=jnp.int32)[None, :]
+    query_wide = jnp.where(
+        slot_match[:, :, None], query_units[:, None, :], jnp.zeros((), jnp.bfloat16)
+    ).reshape(unit_count, slot_width)
+    key_count = both_rows * seq_count
+    key_all = key_in.reshape(key_count, slot_width)
+    value_all = value_in.reshape(key_count, slot_width)
+    scores = (
+        jnp.einsum("uw,kw->uk", query_wide, key_all, preferred_element_type=jnp.float32)
+        * score_scale
+    )
+    local_row = jnp.arange(both_rows, dtype=jnp.int32)[:, None]
+    text_slot = targets[None, :] * text_rows + local_row - img_rows
+    valid = ((local_row < img_rows) | (text_slot < length)).reshape(-1)
+    scores = jnp.where(valid[None, :], scores, -1e30)
+    row_top = jnp.max(scores, -1, keepdims=True)
+    weights = jnp.exp(scores - row_top)
+    total = jnp.sum(weights, -1, keepdims=True)
+    mixed = jnp.dot(
+        weights.astype(jnp.bfloat16), value_all, preferred_element_type=jnp.float32
+    ).reshape(unit_count, head_span, HEAD_DIM)
+    picked = jnp.sum(jnp.where(slot_match[:, :, None], mixed, 0.0), 1)
+    unit_out = (picked / total).astype(jnp.bfloat16)
+    placed = lax.dynamic_update_slice_in_dim(
+        jnp.zeros((head_span * img_all, HEAD_DIM), jnp.bfloat16), unit_out, offset, 0
+    )
+    going = (
+        placed.reshape(head_span, seq_count, img_rows, HEAD_DIM)
+        .transpose(2, 1, 0, 3)
+        .reshape(img_rows, seq_count, slot_width)
+    )
+    coming = lax.all_to_all(going, "seq", split_axis=1, concat_axis=1, tiled=True)
+    owner = (slot_heads[:, :, None] == jnp.arange(HEADS, dtype=jnp.int32)[None, None, :]).astype(
+        jnp.bfloat16
+    )
+    attended = (
+        jnp.einsum(
+            "rjsd,jsh->rhd",
+            coming.reshape(img_rows, seq_count, head_span, HEAD_DIM),
+            owner,
+            preferred_element_type=jnp.float32,
+        )
+        .reshape(img_rows, width)
+        .astype(jnp.bfloat16)
+    )
+    return jnp.dot(attended, w_out, preferred_element_type=jnp.float32)
 
 
 def body(
@@ -241,92 +531,16 @@
 ):
     img_rows = queries.shape[1]
     text_rows = text_keys.shape[1]
-    both_rows = img_rows + text_rows
     width = queries.shape[2]
     length = text_len[0]
-    score_scale = HEAD_DIM ** (-0.5)
-    key_rows = jnp.concatenate([image_keys[0], text_keys[0]], 0)
-    value_rows = jnp.concatenate([image_values[0], text_values[0]], 0)
     seq_count = lax.axis_size("seq")
-    img_all = img_rows * seq_count
-    unit_count = HEADS * img_rows
-    head_span = min(HEADS, (unit_count - 1) // img_all + 2)
-    slot_width = head_span * HEAD_DIM
-    targets = jnp.arange(seq_count, dtype=jnp.int32)
-    first_head = targets * unit_count // img_all
-    slot_heads = first_head[:, None] + jnp.arange(head_span, dtype=jnp.int32)[None, :]
-
-    def spread(rows):
-        parts = []
-        for target in range(seq_count):
-            lead_head = target * unit_count // img_all
-            for slot in range(lead_head, lead_head + head_span):
-                head = min(slot, HEADS - 1)
-                parts.append(rows[:, head * HEAD_DIM : (head + 1) * HEAD_DIM])
-        return jnp.concatenate(parts, 1).reshape(rows.shape[0], seq_count, slot_width)
-
-    query_in, key_in, value_in = (
-        lax.all_to_all(spread(queries[0]), "seq", split_axis=1, concat_axis=1, tiled=True),
-        lax.all_to_all(spread(key_rows), "seq", split_axis=1, concat_axis=1, tiled=True),
-        lax.all_to_all(spread(value_rows), "seq", split_axis=1, concat_axis=1, tiled=True),
-    )
-    myself = lax.axis_index("seq")
-    lead = myself * unit_count // img_all
-    offset = myself * unit_count - lead * img_all
-    query_flat = (
-        query_in.reshape(img_rows, seq_count, head_span, HEAD_DIM)
-        .transpose(2, 1, 0, 3)
-        .reshape(head_span * img_all, HEAD_DIM)
-    )
-    query_units = lax.dynamic_slice_in_dim(query_flat, offset, unit_count, 0)
-    unit_slot = (offset + jnp.arange(unit_count, dtype=jnp.int32)) // img_all
-    slot_match = unit_slot[:, None] == jnp.arange(head_span, dtype=jnp.int32)[None, :]
-    query_wide = jnp.where(
-        slot_match[:, :, None], query_units[:, None, :], jnp.zeros((), jnp.bfloat16)
-    ).reshape(unit_count, slot_width)
-    key_count = both_rows * seq_count
-    key_all = key_in.reshape(key_count, slot_width)
-    value_all = value_in.reshape(key_count, slot_width)
-    scores = (
-        jnp.einsum("uw,kw->uk", query_wide, key_all, preferred_element_type=jnp.float32)
-        * score_scale
-    )
-    local_row = jnp.arange(both_rows, dtype=jnp.int32)[:, None]
-    text_slot = targets[None, :] * text_rows + local_row - img_rows
-    valid = ((local_row < img_rows) | (text_slot < length)).reshape(-1)
-    scores = jnp.where(valid[None, :], scores, -1e30)
-    row_top = jnp.max(scores, -1, keepdims=True)
-    weights = jnp.exp(scores - row_top)
-    total = jnp.sum(weights, -1, keepdims=True)
-    mixed = jnp.dot(
-        weights.astype(jnp.bfloat16), value_all, preferred_element_type=jnp.float32
-    ).reshape(unit_count, head_span, HEAD_DIM)
-    picked = jnp.sum(jnp.where(slot_match[:, :, None], mixed, 0.0), 1)
-    unit_out = (picked / total).astype(jnp.bfloat16)
-    placed = lax.dynamic_update_slice_in_dim(
-        jnp.zeros((head_span * img_all, HEAD_DIM), jnp.bfloat16), unit_out, offset, 0
-    )
-    going = (
-        placed.reshape(head_span, seq_count, img_rows, HEAD_DIM)
-        .transpose(2, 1, 0, 3)
-        .reshape(img_rows, seq_count, slot_width)
-    )
-    coming = lax.all_to_all(going, "seq", split_axis=1, concat_axis=1, tiled=True)
-    owner = (slot_heads[:, :, None] == jnp.arange(HEADS, dtype=jnp.int32)[None, None, :]).astype(
-        jnp.bfloat16
-    )
-    attended = (
-        jnp.einsum(
-            "rjsd,jsh->rhd",
-            coming.reshape(img_rows, seq_count, head_span, HEAD_DIM),
-            owner,
-            preferred_element_type=jnp.float32,
+    if seq_count == 16 and (img_rows, text_rows, width) == (32, 4, 19 * PAIR):
+        projected = attend_16(
+            queries[0], image_keys[0], image_values[0], text_keys[0], text_values[0], w_out, length
         )
-        .reshape(img_rows, width)
-        .astype(jnp.bfloat16)
-    )
+    else:
+        projected = attend_any(queries, image_keys, image_values, text_keys, text_values, w_out, length)
     mods = modulation[0]
-    projected = jnp.dot(attended, w_out, preferred_element_type=jnp.float32)
     middle = hidden_in[0].astype(jnp.float32) + mods[0] * projected
     normed = (layer_norm(middle) * (1.0 + mods[2]) + mods[1]).astype(jnp.bfloat16)
     if seq_count == 16 and img_rows == 32:

time: 142 us -> 103 us (0.73)
  Pallas kernels: 60.2 us -> 91.3 us
  starting transfers between devices: 25.2 us -> 1.54 us
  waiting for transfers between devices: 19.4 us -> 0.01 us
  local copies, waits for them, and re-layouts: 16.7 us -> 3.68 us
  matrix products: 10.3 us -> 0.27 us
  other arithmetic: 6.14 us -> 2.62 us
    pallas_call x0 -> x1, Pallas kernels: none -> 29 us  [attend_16(): pl.pallas_call(functools.partial(attend_kernel, rows), out_shape=jax.Shap...]
    all_to_all x4 -> x0, starting transfers between devices: 23.6 us -> none  [the longest x1 7.41 us: body(): lax.all_to_all(spread(queries[0]), 'seq', split_axis=1, concat_axis=1, ti...]
    all_to_all x4 -> x0, waiting for transfers between devices: 19.4 us -> none  [the longest x1 7.65 us: body(): lax.all_to_all(spread(key_rows), 'seq', split_axis=1, concat_axis=1, tile...]
    dot_general x4 -> x0, matrix products: 10 us -> none  [the longest x1 6.43 us: body(): projected = jnp.dot(attended, w_out, preferred_element_type=jnp.float32)]
    reshape x9 -> x0, local copies, waits for them, and re-layouts: 6.1 us -> none  [the longest x5 2.38 us: spread(): jnp.concatenate(parts, 1).reshape(rows.shape[0], seq_count, slot_width)]
    unnamed x21 -> x10, local copies, waits for them, and re-layouts: 4.36 us -> 0.03 us
    concatenate x3 -> x1, local copies, waits for them, and re-layouts: 0.28 us -> 3.64 us  [attend_16(): jnp.concatenate([queries, image_keys, image_values, text_keys, text_value...]
    concatenate x8 -> x0, other arithmetic: 3.27 us -> none  [the longest x4 2.93 us: body(): key_rows = jnp.concatenate([image_keys[0], text_keys[0]], 0)]
  transfers between devices with their start and end apart: 5 -> 1, of which waited for: 4 -> 0; matrix products, arithmetic and copies ran while one was open for 8% -> 0% of each run, Pallas kernels for 0% -> 0%
where the time goes in v2:
time: 103 us; the launch traced here: 102 us
  Pallas kernels  91.3 us (89%)
  local copies, waits for them, and re-layouts  3.68 us (4%)
  between operations  2.8 us (3%)
  other arithmetic  2.62 us (3%)
  starting transfers between devices  1.54 us (1%)
    pallas_call x1, Pallas kernels, ffn_16(): pl.pallas_call(functools.partial(ffn_kernel, ca), out_shape=jax.ShapeDtyp...  62.3 us
    pallas_call x1, Pallas kernels, attend_16(): pl.pallas_call(functools.partial(attend_kernel, rows), out_shape=jax.Shap...  29 us
    concatenate x1, local copies, waits for them, and re-layouts, attend_16(): jnp.concatenate([queries, image_keys, image_values, text_keys, text_value...  3.64 us
  transfers between devices with their start and end apart: 1, of which 0 were waited for; matrix products, arithmetic and copies ran while one was open for 0% of the time, Pallas kernels for 0%

profile of v2, /device:TPU:1, one launch (start us, length us, event | category | flops | bytes accessed | tf_op | source)
XLA Modules:
  0.0 102.2 jit_solution(6109300352166885230)
XLA Ops:
  0.6 0.0 copy-start
  0.6 1.0 add_reduce_fusion
  2.3 3.6 %concatenate.3.st_ref = bf16[112,2432]{1,0:T(8,128)(2,1)S(1)} concatenate(bf16[32,2432]{1,0:T(8,128)(2,1)} %bitcast.25, bf16[32,2432]{1,0:T(8,128)(2,1)} %bitcast.26, bf16[32,2432]{1,0:T(8,128)(2,1)} %bitcast.27, bf16[4,2432]{1,0:T(4,128)(2,1)} %bitcast.28, bf16[4,2432]{1,0:T(4,128)(2,1)} %bitcast.29, bf16[8,2432]{1,0:T(8,128)(2,1)S(1)} %broadcast_in_dim.10), dimensions={0} | concatenate | bytes 1089536 | tf_op jit(solution)/shard_map/concatenate | solution.py:369
  6.0 0.0 copy-start.3
  6.0 0.0 copy-start.1
  6.0 0.0 copy-start.2
  6.0 29.0 %shard_map.158 = f32[32,2432]{1,0:T(8,128)S(1)} custom-call(bf16[112,2432]{1,0:T(8,128)(2,1)S(1)} %concatenate.3.st_ref, f32[1,576]{1,0:T(1,128)S(1)} %compare_select_fusion.bias_ref, bf16[2432,2432]{1,0:T(8,128)(2,1)} %wo_ref.1), custom_call_target="tpu_custom_call" | custom-call | flops 378535936 | bytes 11829248 | tf_op jit(solution)/shard_map/pallas_call | solution.py:376
  35.0 0.0 copy-done.3
  35.0 0.2 fusion.1
  35.1 0.2 multiply_reduce_fusion.1
  35.4 0.1 add_convert_fusion.1.norm_ref
  35.5 0.0 copy-done.1
  35.5 0.0 copy-done.2
  35.5 62.3 %shard_map.159 = f32[32,2432]{1,0:T(8,128)S(1)} custom-call(bf16[32,2432]{1,0:T(8,128)(2,1)S(1)} %add_convert_fusion.1.norm_ref, bf16[608,2432]{1,0:T(8,128)(2,1)S(1)} %bitcast.24, bf16[608,2432]{1,0:T(8,128)(2,1)S(1)} %copy-done.2), custom_call_target="tpu_custom_call" | custom-call | flops 3028287488 | bytes 5914624 | tf_op jit(solution)/shard_map/pallas_call | solution.py:167
  97.9 0.0 copy-start.4
  97.9 0.2 fusion.2
  98.1 0.2 multiply_reduce_fusion
  98.3 0.0 copy-done
  98.3 0.3 fusion
  98.6 1.5 %collective-permute-start = (f32[32,64]{1,0:T(8,128)S(1)}, f32[32,64]{1,0:T(8,128)S(1)}, u32[]{:S(2)}, u32[]{:S(2)}) collective-permute-start(f32[32,64]{1,0:T(8,128)S(1)} %fusion), channel_id=1, source_target_pairs={{0,16},{16,0},{1,17},{17,1},{2,18},{18,2},{3,19},{19,3},{4,20},{20... | collective-permute-start | bytes 24584 | tf_op jit(solution)/shard_map/ppermute | solution.py:22
  101.5 0.0 collective-permute-done
  101.5 0.0 copy-done.4
  101.5 0.7 multiply_add_fusion.1
  (6 shorter events, 0.0 us)
Async XLA Ops:
  0.6 97.7 %copy-start = (bf16[2432,64]{0,1:T(8,128)(2,1)S(1)}, bf16[2432,64]{0,1:T(8,128)(2,1)}, u32[]{:S(2)}) copy-start(bf16[2432,64]{0,1:T(8,128)(2,1)} %param.25) | copy-start | bytes 933892
  6.0 29.0 %copy-start.3 = (bf16[1,32,2432]{2,1,0:T(8,128)(2,1)S(1)}, bf16[1,32,2432]{2,1,0:T(8,128)(2,1)}, u32[]{:S(2)}) copy-start(bf16[1,32,2432]{2,1,0:T(8,128)(2,1)} %param.20) | copy-start | bytes 466948
  6.0 29.6 %copy-start.1 = (bf16[2432,608]{0,1:T(8,128)(2,1)S(1)}, bf16[2432,608]{0,1:T(8,128)(2,1)}, u32[]{:S(2)}) copy-start(bf16[2432,608]{0,1:T(8,128)(2,1)} %param.23) | copy-start | bytes 8871940
  6.0 29.6 %copy-start.2 = (bf16[608,2432]{1,0:T(8,128)(2,1)S(1)}, bf16[608,2432]{1,0:T(8,128)(2,1)}, u32[]{:S(2)}) copy-start(bf16[608,2432]{1,0:T(8,128)(2,1)} %down_ref.1) | copy-start | bytes 8871940
  97.9 3.7 %copy-start.4 = (f32[32,32]{1,0:T(8,128)S(1)}, f32[32,32]{1,0:T(8,128)}, u32[]{:S(2)}) copy-start(f32[32,32]{1,0:T(8,128)} %param.26) | copy-start | bytes 12292
  98.6 2.9 %collective-permute-start = (f32[32,64]{1,0:T(8,128)S(1)}, f32[32,64]{1,0:T(8,128)S(1)}, u32[]{:S(2)}, u32[]{:S(2)}) collective-permute-start(f32[32,64]{1,0:T(8,128)S(1)} %fusion), channel_id=1, source_target_pairs={{0,16},{16,0},{1,17},{17,1},{2,18},{18,2},{3,19},{19,3},{4,20},{20... | collective-permute-start | bytes 24584 | tf_op jit(solution)/shard_map/ppermute | solution.py:22

commit v3 on v2

--- a/solution.py
+++ b/solution.py
@@ -42,7 +42,7 @@
     my = lax.rem(me // 2, 2)
     xn = mz * 4 + my * 2 + (1 - mx)
     yn = mz * 4 + (1 - my) * 2 + mx
-    zs = [lax.rem(mz + k, 4) for k in range(4)]
+    zs = [mz, mz + 1 - 2 * lax.rem(mz, 2), lax.rem(mz + 2, 4), 3 - mz]
     zn = [z * 4 + my * 2 + mx for z in zs]
     width = norm_ref.shape[1]
     cols = (pl.ds(0, ca), pl.ds(ca, width - ca))
@@ -73,7 +73,7 @@
 
     g[0, mz] = norm_ref[...]
     pl.semaphore_wait(barrier, len(peers))
-    for k in (2, 1, 3):
+    for k in (1, 3, 2):
         send(norm_ref, g.at[0, mz], gsem.at[0, mz], zn[k])
     send(norm_ref, g.at[1, mz], gsem.at[1, mz], xn)
     send(norm_ref, g.at[2, mz], gsem.at[2, mz], yn)
@@ -115,8 +115,6 @@
     send(pb.at[2, :, :, a], ry0, dsem.at[1], yn)
     pf[1, :, :, a] = down(hid1, 0)
     pf[2, :, :, b] = down(hid2, 1)
-    pf[0, :, :, a] = down(hid0, 0)
-    pf[0, :, :, b] = down(hid0, 1)
     for z in zs:
         arrived(g.at[3, z, :, a], gsem.at[3, z])
         arrived(g.at[3, z, :, b], gsem.at[4, z])
@@ -128,6 +126,8 @@
     pb[3, :, :, b] = down(hid3, 1).astype(jnp.bfloat16)
     for k in order:
         send(pb.at[3, zs[k], :, b], rx1.at[zs[k]], esem.at[1, zs[k]], xn)
+    pf[0, :, :, a] = down(hid0, 0)
+    pf[0, :, :, b] = down(hid0, 1)
     for k in order:
         z = zs[k]
         arrived(ry1.at[z], esem.at[0, z])
@@ -209,7 +209,7 @@
 
 
 def attend_kernel(
-    rows, st_ref, bias_ref, wo_ref, out_ref, wo, land, kb, vb, res, att, wsem, ssem, xsem, rsem, osem, asem, lsem
+    rows, q_ref, k_ref, v_ref, text_ref, bias_ref, wo_ref, out_ref, st_ref, wo, land, kb, vb, res, att, wsem, ssem, xsem, rsem, osem, asem, lsem
 ):
     me = lax.axis_index("seq")
     mesh_id = pl.DeviceIdType.MESH
@@ -226,10 +226,15 @@
             src_ref=src, dst_ref=dst, send_sem=sent, recv_sem=got, device_id={"seq": peer}, device_id_type=mesh_id
         )
 
+    stack = [
+        pltpu.make_async_copy(ref, st_ref.at[pl.ds(i * rows, ref.shape[0])], wsem.at[i + 1])
+        for i, ref in enumerate((q_ref, k_ref, v_ref, text_ref))
+    ]
+    for copy in stack:
+        copy.start()
     load = pltpu.make_async_copy(wo_ref, wo, wsem.at[0])
     load.start()
     own = pltpu.make_async_copy(st_ref.at[:, lanes(me)], land.at[0, me], lsem.at[0])
-    own.start()
     barrier = pltpu.get_barrier_semaphore()
 
     def greet(k, c):
@@ -237,6 +242,9 @@
         return c
 
     lax.fori_loop(1, 16, greet, 0)
+    for copy in stack:
+        copy.wait()
+    own.start()
     pl.semaphore_wait(barrier, 15)
 
     def extra_in(e, owner):
@@ -286,23 +294,23 @@
         low = lax.broadcasted_iota(jnp.int32, (4 * rows, PAIR), 1) < HEAD_DIM
 
         def chunk(c, carry):
-            q = land[u, pl.ds(c * 4, 4), 0:rows, :].reshape(4 * rows, PAIR)
             made = []
-            for head in range(2):
-                mine = low if head == 0 else jnp.logical_not(low)
-                q_one = jnp.where(mine, q, jnp.zeros_like(q))
+            for part in range(2):
+                q = land[u, pl.ds(c * 8 + part * 4, 4), 0:rows, :].reshape(4 * rows, PAIR)
+                none = jnp.zeros_like(q)
+                q_two = jnp.concatenate([jnp.where(low, q, none), jnp.where(low, none, q)], 0)
                 scores = lax.dot_general(
-                    q_one, kb[...], (((1,), (1,)), ((), ())), preferred_element_type=jnp.float32
+                    q_two, kb[...], (((1,), (1,)), ((), ())), preferred_element_type=jnp.float32
                 ) * (HEAD_DIM ** (-0.5))
                 scores = scores + bias_ref[...]
                 top = jnp.max(scores, -1, keepdims=True)
                 weights = jnp.exp(scores - top)
                 total = jnp.sum(weights, -1, keepdims=True)
-                mixed = jnp.dot(weights.astype(jnp.bfloat16), vb[...], preferred_element_type=jnp.float32)
-                made.append(mixed / total)
-            both = jnp.where(low, made[0], made[1]).astype(jnp.bfloat16)
-            for j in range(4):
-                dst = c * 4 + j
+                mixed = jnp.dot(weights.astype(jnp.bfloat16), vb[...], preferred_element_type=jnp.float32) / total
+                made.append(jnp.where(low, mixed[: 4 * rows], mixed[4 * rows :]).astype(jnp.bfloat16))
+            both = jnp.concatenate(made, 0)
+            for j in range(8):
+                dst = c * 8 + j
                 res[u, dst] = both[j * rows : (j + 1) * rows, :]
 
                 @pl.when(dst != me)
@@ -315,7 +323,7 @@
 
             return carry
 
-        lax.fori_loop(0, 4, chunk, 0)
+        lax.fori_loop(0, 2, chunk, 0)
 
     unit(0, me, own)
     for e, owner in enumerate(EXTRA):
@@ -366,10 +374,8 @@
 def attend_16(queries, image_keys, image_values, text_keys, text_values, w_out, length):
     rows, width = queries.shape
     half = jnp.bfloat16
-    stacked = jnp.concatenate(
-        [queries, image_keys, image_values, text_keys, text_values, jnp.zeros((8, width), half)], 0
-    )
-    deep = stacked.shape[0]
+    text = jnp.concatenate([text_keys, text_values, jnp.zeros((8, width), half)], 0)
+    deep = 3 * rows + text.shape[0]
     key = jnp.arange(576, dtype=jnp.int32)
     bias = jnp.where(key - 512 < length, 0.0, -1e30).astype(jnp.float32)[None, :]
     pairs = width // PAIR
@@ -377,19 +383,23 @@
         functools.partial(attend_kernel, rows),
         out_shape=jax.ShapeDtypeStruct((rows, width), jnp.float32),
         in_specs=[
-            pl.BlockSpec(memory_space=pltpu.VMEM),
+            pl.BlockSpec(memory_space=pl.ANY),
+            pl.BlockSpec(memory_space=pl.ANY),
+            pl.BlockSpec(memory_space=pl.ANY),
+            pl.BlockSpec(memory_space=pl.ANY),
             pl.BlockSpec(memory_space=pltpu.VMEM),
             pl.BlockSpec(memory_space=pl.ANY),
         ],
         out_specs=pl.BlockSpec(memory_space=pltpu.VMEM),
         scratch_shapes=[
+            pltpu.VMEM((deep, width), half),
             pltpu.VMEM((width, width), half),
             pltpu.VMEM((2, 16, deep, PAIR), half),
             pltpu.VMEM((576, PAIR), half),
             pltpu.VMEM((576, PAIR), half),
             pltpu.VMEM((2, 16, rows, PAIR), half),
             pltpu.VMEM((rows, width), half),
-            pltpu.SemaphoreType.DMA((1,)),
+            pltpu.SemaphoreType.DMA((5,)),
             pltpu.SemaphoreType.DMA((16,)),
             pltpu.SemaphoreType.DMA((len(EXTRA),)),
             pltpu.SemaphoreType.DMA((2, 16)),
@@ -403,7 +413,7 @@
         compiler_params=pltpu.CompilerParams(
             collective_id=1, has_side_effects=True, vmem_limit_bytes=44 * 2**20
         ),
-    )(stacked, bias, w_out)
+    )(queries, image_keys, image_values, text, bias, w_out)
 
 
 def ffn_any(normed, w_up, w_down):

time: 103 us -> 96.2 us (0.934)
  Pallas kernels: 91.3 us -> 80.4 us
  starting transfers between devices: 1.54 us -> 6.1 us
    pallas_call x1, Pallas kernels: 62.3 us -> 51.4 us  [ffn_16(): pl.pallas_call(functools.partial(ffn_kernel, ca), out_shape=jax.ShapeDtyp...]
    ppermute x1, starting transfers between devices: 1.54 us -> 6.1 us  [partner_2(): return lax.ppermute(value, axis, pairs)]
    concatenate x1, local copies, waits for them, and re-layouts: 3.64 us -> 0.08 us  [attend_16(): jnp.concatenate([text_keys, text_values, jnp.zeros((8, width), half)], 0)]
    unnamed x10 -> x16, local copies, waits for them, and re-layouts: 0.03 us -> 2.76 us
where the time goes in v3:
time: 96.2 us; the launch traced here: 95.9 us
  Pallas kernels  80.4 us (84%)
  starting transfers between devices  6.1 us (6%)
  other arithmetic  3.47 us (4%)
  local copies, waits for them, and re-layouts  2.84 us (3%)
  between operations  2.8 us (3%)
    pallas_call x1, Pallas kernels, ffn_16(): pl.pallas_call(functools.partial(ffn_kernel, ca), out_shape=jax.ShapeDtyp...  51.4 us
    pallas_call x1, Pallas kernels, attend_16(): pl.pallas_call(functools.partial(attend_kernel, rows), out_shape=jax.Shap...  29 us
    ppermute x1, starting transfers between devices, partner_2(): return lax.ppermute(value, axis, pairs)  6.1 us
    unnamed x16, local copies, waits for them, and re-layouts  2.76 us
  transfers between devices with their start and end apart: 1, of which 0 were waited for; matrix products, arithmetic and copies ran while one was open for 0% of the time, Pallas kernels for 0%

profile of v3, /device:TPU:1, one launch (start us, length us, event | category | flops | bytes accessed | tf_op | source)
XLA Modules:
  0.0 95.9 jit_solution(4353732694881875582)
XLA Ops:
  0.6 0.0 copy-start
  0.6 1.0 %add_reduce_fusion = (f32[2432]{0:T(1024)S(1)}, f32[2432]{0:T(1024)S(1)}, f32[2432]{0:T(1024)S(1)}, f32[2432]{0:T(1024)S(1)}, f32[2432]{0:T(1024)S(1)}, /*index=5*/f32[2432]{0:T(1024)S(1)}) fusion(f32[1,6,2432]{2,0,1:T(1,128)} %param.21), kind=kLoop, calls=%fused_computation.12 | loop fusion | flops 4864 | bytes 116736 | tf_op jit(solution)/shard_map/add | solution.py:561
  2.3 0.1 pad.2.clone
  2.4 0.8 maximum_maximum_fusion.text_ref
  3.2 0.0 copy-start.1
  3.2 0.9 copy-done.1
  4.1 0.0 copy-start.2
  4.1 0.9 copy-done.2
  5.0 0.0 copy-start.3
  5.0 0.9 copy-done.3
  6.0 0.0 copy-start.6
  6.0 0.0 copy-start.4
  6.0 0.0 copy-start.5
  6.0 29.0 %shard_map.158 = f32[32,2432]{1,0:T(8,128)S(1)} custom-call(bf16[32,2432]{1,0:T(8,128)(2,1)S(1)} %bitcast.24, bf16[32,2432]{1,0:T(8,128)(2,1)S(1)} %bitcast.25, bf16[32,2432]{1,0:T(8,128)(2,1)S(1)} %bitcast.26, bf16[16,2432]{1,0:T(8,128)(2,1)S(1)} %maximum_maximum_fusion.text_ref, f32[1,576]{1,0:T(1,128)S(1)} %compare_select_fusion.bias_ref, ...), custom_call_target="tpu_custom_call" | custom-call | flops 378535936 | bytes 11829248 | tf_op jit(solution)/shard_map/pallas_call | solution.py:382
  35.0 0.0 copy-done.6
  35.0 0.2 fusion.1
  35.1 0.2 multiply_reduce_fusion.1
  35.4 0.1 add_convert_fusion.1.norm_ref
  35.5 0.0 copy-done.4
  35.5 0.0 copy-done.5
  35.5 51.4 %shard_map.159 = f32[32,2432]{1,0:T(8,128)S(1)} custom-call(bf16[32,2432]{1,0:T(8,128)(2,1)S(1)} %add_convert_fusion.1.norm_ref, bf16[608,2432]{1,0:T(8,128)(2,1)S(1)} %bitcast.27, bf16[608,2432]{1,0:T(8,128)(2,1)S(1)} %copy-done.5), custom_call_target="tpu_custom_call" | custom-call | flops 3028287488 | bytes 5914624 | tf_op jit(solution)/shard_map/pallas_call | solution.py:167
  87.0 0.0 copy-start.7
  87.0 0.2 fusion.2
  87.2 0.2 multiply_reduce_fusion
  87.4 0.0 copy-done
  87.4 0.3 fusion
  87.7 6.1 %collective-permute-start = (f32[32,64]{1,0:T(8,128)S(1)}, f32[32,64]{1,0:T(8,128)S(1)}, u32[]{:S(2)}, u32[]{:S(2)}) collective-permute-start(f32[32,64]{1,0:T(8,128)S(1)} %fusion), channel_id=1, source_target_pairs={{0,16},{16,0},{1,17},{17,1},{2,18},{18,2},{3,19},{19,3},{4,20},{20... | collective-permute-start | bytes 24584 | tf_op jit(solution)/shard_map/ppermute | solution.py:22
  95.2 0.0 collective-permute-done
  95.2 0.0 copy-done.7
  95.2 0.7 multiply_add_fusion.1
  (6 shorter events, 0.0 us)
Async XLA Ops:
  0.6 86.8 %copy-start = (bf16[2432,64]{0,1:T(8,128)(2,1)S(1)}, bf16[2432,64]{0,1:T(8,128)(2,1)}, u32[]{:S(2)}) copy-start(bf16[2432,64]{0,1:T(8,128)(2,1)} %param.25) | copy-start | bytes 933892
  3.2 0.9 copy-start.1
  4.1 0.9 copy-start.2
  5.0 0.9 copy-start.3
  6.0 29.0 %copy-start.6 = (bf16[1,32,2432]{2,1,0:T(8,128)(2,1)S(1)}, bf16[1,32,2432]{2,1,0:T(8,128)(2,1)}, u32[]{:S(2)}) copy-start(bf16[1,32,2432]{2,1,0:T(8,128)(2,1)} %param.20) | copy-start | bytes 466948
  6.0 29.6 %copy-start.4 = (bf16[2432,608]{0,1:T(8,128)(2,1)S(1)}, bf16[2432,608]{0,1:T(8,128)(2,1)}, u32[]{:S(2)}) copy-start(bf16[2432,608]{0,1:T(8,128)(2,1)} %param.23) | copy-start | bytes 8871940
  6.0 29.6 %copy-start.5 = (bf16[608,2432]{1,0:T(8,128)(2,1)S(1)}, bf16[608,2432]{1,0:T(8,128)(2,1)}, u32[]{:S(2)}) copy-start(bf16[608,2432]{1,0:T(8,128)(2,1)} %down_ref.1) | copy-start | bytes 8871940
  87.0 8.2 %copy-start.7 = (f32[32,32]{1,0:T(8,128)S(1)}, f32[32,32]{1,0:T(8,128)}, u32[]{:S(2)}) copy-start(f32[32,32]{1,0:T(8,128)} %param.26) | copy-start | bytes 12292
  87.7 7.5 %collective-permute-start = (f32[32,64]{1,0:T(8,128)S(1)}, f32[32,64]{1,0:T(8,128)S(1)}, u32[]{:S(2)}, u32[]{:S(2)}) collective-permute-start(f32[32,64]{1,0:T(8,128)S(1)} %fusion), channel_id=1, source_target_pairs={{0,16},{16,0},{1,17},{17,1},{2,18},{18,2},{3,19},{19,3},{4,20},{20... | collective-permute-start | bytes 24584 | tf_op jit(solution)/shard_map/ppermute | solution.py:22

commit v4 on v3

--- a/solution.py
+++ b/solution.py
@@ -199,12 +199,12 @@
             flops=4 * 16 * rows * width * hidden, bytes_accessed=4 * width * hidden, transcendentals=16 * rows * hidden
         ),
         compiler_params=pltpu.CompilerParams(
-            collective_id=0, has_side_effects=True, vmem_limit_bytes=44 * 2**20
+            collective_id=0, has_side_effects=True, vmem_limit_bytes=58 * 2**20
         ),
     )(normed, w_up.T, w_down)
 
 
-EXTRA = (5, 8, 6)
+EXTRA = ((16, 0, 5), (16, 1, 8), (17, 0, 6), (17, 1, 11), (18, 0, 4), (18, 1, 9))
 PAIR = 2 * HEAD_DIM
 
 
@@ -247,11 +247,11 @@
     own.start()
     pl.semaphore_wait(barrier, 15)
 
-    def extra_in(e, owner):
-        return remote(st_ref.at[:, lanes(16 + e)], land.at[1, me], xsem.at[e], rsem.at[1, me], owner)
-
-    def extra_own(e):
-        return pltpu.make_async_copy(st_ref.at[:, lanes(16 + e)], land.at[1, me], lsem.at[1])
+    def extra_in(e, pair, owner):
+        return remote(st_ref.at[:, lanes(pair)], land.at[1, me], xsem.at[e], rsem.at[1, me], owner)
+
+    def extra_own(pair):
+        return pltpu.make_async_copy(st_ref.at[:, lanes(pair)], land.at[1, me], lsem.at[1])
 
     def pair_in(k):
         peer = peer_of(k)
@@ -262,20 +262,20 @@
         return c
 
     lax.fori_loop(1, 16, go, 0)
-    for e, owner in enumerate(EXTRA):
+    for e, (pair, part, owner) in enumerate(EXTRA):
 
         @pl.when(me != owner)
         def _():
-            extra_in(e, owner).start()
+            extra_in(e, pair, owner).start()
 
         @pl.when(me == owner)
         def _():
-            extra_own(e).start()
+            extra_own(pair).start()
 
     def back(u, dst, pair):
         return remote(res.at[u, dst], att.at[:, lanes(pair)], osem.at[u, dst], asem.at[pair], dst)
 
-    def unit(u, pair, local):
+    def unit(u, pair, local, first, last):
         def arrive(k, c):
             src = peer_of(k)
             remote(land.at[u, src], land.at[u, src], ssem.at[0], rsem.at[u, src], src).wait_recv()
@@ -323,14 +323,14 @@
 
             return carry
 
-        lax.fori_loop(0, 2, chunk, 0)
-
-    unit(0, me, own)
-    for e, owner in enumerate(EXTRA):
+        lax.fori_loop(first, last, chunk, 0)
+
+    unit(0, me, own, 0, 2)
+    for e, (pair, part, owner) in enumerate(EXTRA):
 
         @pl.when(me == owner)
         def _():
-            unit(1, 16 + e, extra_own(e))
+            unit(1, pair, extra_own(pair), part, part + 1)
 
     def home(pair, src):
         spot = att.at[:, lanes(pair)]
@@ -341,11 +341,11 @@
         return c
 
     lax.fori_loop(1, 16, collect, 0)
-    for e, owner in enumerate(EXTRA):
-
-        @pl.when(me != owner)
+    for e, (pair, part, owner) in enumerate(EXTRA):
+
+        @pl.when((me != owner) & (me // 8 == part))
         def _():
-            home(16 + e, owner)
+            home(pair, owner)
 
     load.wait()
     out_ref[...] = jnp.dot(att[...], wo[...], preferred_element_type=jnp.float32)
@@ -356,19 +356,22 @@
         return c
 
     lax.fori_loop(1, 16, finish, 0)
-    for e, owner in enumerate(EXTRA):
+    for e, (pair, part, owner) in enumerate(EXTRA):
 
         @pl.when(me != owner)
         def _():
-            extra_in(e, owner).wait_send()
+            extra_in(e, pair, owner).wait_send()
 
         @pl.when(me == owner)
         def _():
-            def finish_extra(k, c):
-                back(1, peer_of(k), 16 + e).wait_send()
+            def finish_extra(dst, c):
+                @pl.when(dst != me)
+                def _():
+                    back(1, dst, pair).wait_send()
+
                 return c
 
-            lax.fori_loop(1, 16, finish_extra, 0)
+            lax.fori_loop(part * 8, part * 8 + 8, finish_extra, 0)
 
 
 def attend_16(queries, image_keys, image_values, text_keys, text_values, w_out, length):
@@ -411,7 +414,7 @@
             flops=2 * rows * width * width, bytes_accessed=2 * width * width, transcendentals=2 * 512 * 576
         ),
         compiler_params=pltpu.CompilerParams(
-            collective_id=1, has_side_effects=True, vmem_limit_bytes=44 * 2**20
+            collective_id=1, has_side_effects=True, vmem_limit_bytes=58 * 2**20
         ),
     )(queries, image_keys, image_values, text, bias, w_out)
 

time: 96.2 us -> 99.1 us (1.030)
  other arithmetic: 3.47 us -> 9.19 us
  local copies, waits for them, and re-layouts: 2.84 us -> 0.1 us
    unnamed x16 -> x8, local copies, waits for them, and re-layouts: 2.76 us -> 0.02 us
    pallas_call x1, Pallas kernels: 51.4 us -> 49.3 us  [ffn_16(): pl.pallas_call(functools.partial(ffn_kernel, ca), out_shape=jax.ShapeDtyp...]
    reduce_sum x2, other arithmetic: 0.36 us -> 2.27 us  [layer_norm(): centred = values - jnp.mean(values, -1, keepdims=True)]
    convert_element_type x1, other arithmetic: 0.13 us -> 1.75 us  [body(): (layer_norm(middle) * (1.0 + mods[2]) + mods[1]).astype(jnp.bfloat16)]
    pallas_call x1, Pallas kernels: 29 us -> 30.4 us  [attend_16(): pl.pallas_call(functools.partial(attend_kernel, rows), out_shape=jax.Shap...]
where the time goes in v4:
time: 99.1 us; the launch traced here: 98.7 us
  Pallas kernels  79.7 us (80%)
  other arithmetic  9.19 us (9%)
  starting transfers between devices  6.7 us (7%)
  between operations  2.76 us (3%)
    pallas_call x1, Pallas kernels, ffn_16(): pl.pallas_call(functools.partial(ffn_kernel, ca), out_shape=jax.ShapeDtyp...  49.3 us
    pallas_call x1, Pallas kernels, attend_16(): pl.pallas_call(functools.partial(attend_kernel, rows), out_shape=jax.Shap...  30.4 us
    ppermute x1, starting transfers between devices, partner_2(): return lax.ppermute(value, axis, pairs)  6.7 us
    reduce_sum x2, other arithmetic, layer_norm(): centred = values - jnp.mean(values, -1, keepdims=True)  2.27 us
  transfers between devices with their start and end apart: 1, of which 0 were waited for; matrix products, arithmetic and copies ran while one was open for 0% of the time, Pallas kernels for 0%

profile of v4, /device:TPU:1, one launch (start us, length us, event | category | flops | bytes accessed | tf_op | source)
XLA Modules:
  0.0 98.7 jit_solution(13065090774282980089)
XLA Ops:
  0.6 0.0 copy-start
  0.6 1.0 add_reduce_fusion
  2.3 0.6 compare_select_fusion.bias_ref
  2.9 0.1 pad.2.clone
  3.0 1.5 %maximum_maximum_fusion.text_ref = bf16[16,2432]{1,0:T(8,128)(2,1)} fusion(bf16[4,2432]{1,0:T(4,128)(2,1)} %bitcast.27, bf16[4,2432]{1,0:T(4,128)(2,1)} %bitcast.28, bf16[16]{0:T(256)(128)(2,1)S(1)} %pad.2.clone), kind=kLoop, calls=%fused_computation.7 | loop fusion | flops 233472 | bytes 116768 | tf_op jit(solution)/shard_map/concatenate | solution.py:380
  4.4 0.0 copy-start.2
  4.4 30.4 %shard_map.158 = f32[32,2432]{1,0:T(8,128)} custom-call(bf16[32,2432]{1,0:T(8,128)(2,1)} %bitcast.24, bf16[32,2432]{1,0:T(8,128)(2,1)} %bitcast.25, bf16[32,2432]{1,0:T(8,128)(2,1)} %bitcast.26, bf16[16,2432]{1,0:T(8,128)(2,1)} %maximum_maximum_fusion.text_ref, f32[1,576]{1,0:T(1,128)} %compare_select_fusion.bias_ref, bf16[2432,2432]{1,0:T(8,128)(2,1)} %wo_ref.1), custom_call_target="tpu_custom_call" | custom-call | flops 378535936 | bytes 11829248 | tf_op jit(solution)/shard_map/pallas_call | solution.py:385
  34.8 0.0 copy-done.2
  34.8 1.1 %fusion.1 = f32[32]{0:T(128)S(1)} fusion(f32[32,2432]{1,0:T(8,128)} %shard_map.158, f32[2432]{0:T(1024)S(1)} %get-tuple-element.6, bf16[1,32,2432]{2,1,0:T(8,128)(2,1)S(1)} %copy-done.2), kind=kLoop, calls=%fused_computation.21 | loop fusion | flops 311264 | bytes 476800 | tf_op jit(solution)/shard_map/reduce_sum | solution.py:26
  35.9 1.2 %multiply_reduce_fusion.1 = f32[32]{0:T(128)S(1)} fusion(f32[32]{0:T(128)S(1)} %broadcast_multiply_fusion.1, f32[32,2432]{1,0:T(8,128)} %shard_map.158, f32[2432]{0:T(1024)S(1)} %get-tuple-element.6, bf16[1,32,2432]{2,1,0:T(8,128)(2,1)S(1)} %copy-done.2), kind=kLoop, calls=%fused_computation.5 | loop fusion | flops 466912 | bytes 476928 | tf_op jit(solution)/shard_map/reduce_sum | solution.py:27
  37.1 1.8 %add_convert_fusion.1.norm_ref = bf16[32,2432]{1,0:T(8,128)(2,1)} fusion(f32[2432]{0:T(1024)S(1)} %get-tuple-element.3, f32[2432]{0:T(1024)S(1)} %get-tuple-element.4, f32[32]{0:T(128)S(1)} %add_sqrt_fusion.1, f32[32]{0:T(128)S(1)} %broadcast_multiply_fusion.1, f32[32,2432]{1,0:T(8,128)} %shard_map.158, f32[2432]{0:T(1024)S(1)} %get-tuple-element.6, ...), kind=kLoop, calls=%fused_computation.4 | loop fusion | flops 622592 | bytes 652032 | tf_op jit(solution)/shard_map/convert_element_type | solution.py:558
  38.9 0.0 copy-start.1
  38.9 49.3 %shard_map.159 = f32[32,2432]{1,0:T(8,128)} custom-call(bf16[32,2432]{1,0:T(8,128)(2,1)} %add_convert_fusion.1.norm_ref, bf16[608,2432]{1,0:T(8,128)(2,1)} %bitcast.29, bf16[608,2432]{1,0:T(8,128)(2,1)} %down_ref.1), custom_call_target="tpu_custom_call" | custom-call | flops 3028287488 | bytes 5914624 | tf_op jit(solution)/shard_map/pallas_call | solution.py:167
  88.2 0.0 copy-start.3
  88.2 0.0 copy-done.1
  88.2 1.1 %fusion.2 = (f32[32]{0:T(128)S(1)}, f32[32,2432]{1,0:T(8,128)S(1)}) fusion(f32[32,2432]{1,0:T(8,128)} %shard_map.159, f32[2432]{0:T(1024)S(1)} %get-tuple-element.5, f32[32,2432]{1,0:T(8,128)S(1)} %copy-done.1, f32[2432]{0:T(1024)S(1)} %get-tuple-element.6, bf16[1,32,2432]{2,1,0:T(8,128)(2,1)S(1)} %copy-done.2), kind=kLoop, calls=%fused_computation.22 | loop fusion | flops 466912 | bytes 1109120 | tf_op jit(solution)/shard_map/reduce_sum | solution.py:26
  89.4 0.2 multiply_reduce_fusion
  89.6 0.0 copy-done
  89.6 0.3 fusion
  89.9 6.7 %collective-permute-start = (f32[32,64]{1,0:T(8,128)S(1)}, f32[32,64]{1,0:T(8,128)S(1)}, u32[]{:S(2)}, u32[]{:S(2)}) collective-permute-start(f32[32,64]{1,0:T(8,128)S(1)} %fusion), channel_id=1, source_target_pairs={{0,16},{16,0},{1,17},{17,1},{2,18},{18,2},{3,19},{19,3},{4,20},{20... | collective-permute-start | bytes 24584 | tf_op jit(solution)/shard_map/ppermute | solution.py:22
  98.0 0.0 collective-permute-done
  98.0 0.0 copy-done.3
  98.0 0.7 multiply_add_fusion.1
  (5 shorter events, 0.0 us)
Async XLA Ops:
  0.6 89.0 %copy-start = (bf16[2432,64]{0,1:T(8,128)(2,1)S(1)}, bf16[2432,64]{0,1:T(8,128)(2,1)}, u32[]{:S(2)}) copy-start(bf16[2432,64]{0,1:T(8,128)(2,1)} %param.25) | copy-start | bytes 933892
  4.4 30.4 %copy-start.2 = (bf16[1,32,2432]{2,1,0:T(8,128)(2,1)S(1)}, bf16[1,32,2432]{2,1,0:T(8,128)(2,1)}, u32[]{:S(2)}) copy-start(bf16[1,32,2432]{2,1,0:T(8,128)(2,1)} %param.20) | copy-start | bytes 466948
  38.9 49.3 %copy-start.1 = (f32[32,2432]{1,0:T(8,128)S(1)}, f32[32,2432]{1,0:T(8,128)}, u32[]{:S(2)}) copy-start(f32[32,2432]{1,0:T(8,128)} %shard_map.158) | copy-start | bytes 933892
  88.2 9.8 %copy-start.3 = (f32[32,32]{1,0:T(8,128)S(1)}, f32[32,32]{1,0:T(8,128)}, u32[]{:S(2)}) copy-start(f32[32,32]{1,0:T(8,128)} %param.26) | copy-start | bytes 12292
  89.9 8.1 %collective-permute-start = (f32[32,64]{1,0:T(8,128)S(1)}, f32[32,64]{1,0:T(8,128)S(1)}, u32[]{:S(2)}, u32[]{:S(2)}) collective-permute-start(f32[32,64]{1,0:T(8,128)S(1)} %fusion), channel_id=1, source_target_pairs={{0,16},{16,0},{1,17},{17,1},{2,18},{18,2},{3,19},{19,3},{4,20},{20... | collective-permute-start | bytes 24584 | tf_op jit(solution)/shard_map/ppermute | solution.py:22

commit v5 on v4

--- a/solution.py
+++ b/solution.py
@@ -199,7 +199,7 @@
             flops=4 * 16 * rows * width * hidden, bytes_accessed=4 * width * hidden, transcendentals=16 * rows * hidden
         ),
         compiler_params=pltpu.CompilerParams(
-            collective_id=0, has_side_effects=True, vmem_limit_bytes=58 * 2**20
+            collective_id=0, has_side_effects=True, vmem_limit_bytes=44 * 2**20
         ),
     )(normed, w_up.T, w_down)
 
@@ -414,7 +414,7 @@
             flops=2 * rows * width * width, bytes_accessed=2 * width * width, transcendentals=2 * 512 * 576
         ),
         compiler_params=pltpu.CompilerParams(
-            collective_id=1, has_side_effects=True, vmem_limit_bytes=58 * 2**20
+            collective_id=1, has_side_effects=True, vmem_limit_bytes=44 * 2**20
         ),
     )(queries, image_keys, image_values, text, bias, w_out)
 

time: 99.1 us -> 94.4 us (0.953)
  other arithmetic: 9.19 us -> 3.47 us
  local copies, waits for them, and re-layouts: 0.1 us -> 2.84 us
  Pallas kernels: 79.7 us -> 78 us
    unnamed x8 -> x16, local copies, waits for them, and re-layouts: 0.02 us -> 2.76 us
    reduce_sum x2, other arithmetic: 2.27 us -> 0.36 us  [layer_norm(): centred = values - jnp.mean(values, -1, keepdims=True)]
    convert_element_type x1, other arithmetic: 1.75 us -> 0.13 us  [body(): (layer_norm(middle) * (1.0 + mods[2]) + mods[1]).astype(jnp.bfloat16)]
    pallas_call x1, Pallas kernels: 49.3 us -> 48.3 us  [ffn_16(): pl.pallas_call(functools.partial(ffn_kernel, ca), out_shape=jax.ShapeDtyp...]
where the time goes in v5:
time: 94.4 us; the launch traced here: 94.1 us
  Pallas kernels  78 us (83%)
  starting transfers between devices  6.72 us (7%)
  other arithmetic  3.47 us (4%)
  local copies, waits for them, and re-layouts  2.84 us (3%)
  between operations  2.8 us (3%)
    pallas_call x1, Pallas kernels, ffn_16(): pl.pallas_call(functools.partial(ffn_kernel, ca), out_shape=jax.ShapeDtyp...  48.3 us
    pallas_call x1, Pallas kernels, attend_16(): pl.pallas_call(functools.partial(attend_kernel, rows), out_shape=jax.Shap...  29.7 us
    ppermute x1, starting transfers between devices, partner_2(): return lax.ppermute(value, axis, pairs)  6.72 us
    unnamed x16, local copies, waits for them, and re-layouts  2.76 us
  transfers between devices with their start and end apart: 1, of which 0 were waited for; matrix products, arithmetic and copies ran while one was open for 0% of the time, Pallas kernels for 0%

profile of v5, /device:TPU:1, one launch (start us, length us, event | category | flops | bytes accessed | tf_op | source)
XLA Modules:
  0.0 94.1 jit_solution(3221189917516725228)
XLA Ops:
  0.6 0.0 copy-start
  0.6 1.0 %add_reduce_fusion = (f32[2432]{0:T(1024)S(1)}, f32[2432]{0:T(1024)S(1)}, f32[2432]{0:T(1024)S(1)}, f32[2432]{0:T(1024)S(1)}, f32[2432]{0:T(1024)S(1)}, /*index=5*/f32[2432]{0:T(1024)S(1)}) fusion(f32[1,6,2432]{2,0,1:T(1,128)} %param.21), kind=kLoop, calls=%fused_computation.12 | loop fusion | flops 4864 | bytes 116736 | tf_op jit(solution)/shard_map/add | solution.py:564
  2.3 0.1 pad.2.clone
  2.4 0.8 maximum_maximum_fusion.text_ref
  3.2 0.0 copy-start.1
  3.2 0.9 copy-done.1
  4.1 0.0 copy-start.2
  4.1 0.9 copy-done.2
  5.0 0.0 copy-start.3
  5.0 0.9 copy-done.3
  6.0 0.0 copy-start.6
  6.0 0.0 copy-start.4
  6.0 0.0 copy-start.5
  6.0 29.7 %shard_map.158 = f32[32,2432]{1,0:T(8,128)S(1)} custom-call(bf16[32,2432]{1,0:T(8,128)(2,1)S(1)} %bitcast.24, bf16[32,2432]{1,0:T(8,128)(2,1)S(1)} %bitcast.25, bf16[32,2432]{1,0:T(8,128)(2,1)S(1)} %bitcast.26, bf16[16,2432]{1,0:T(8,128)(2,1)S(1)} %maximum_maximum_fusion.text_ref, f32[1,576]{1,0:T(1,128)S(1)} %compare_select_fusion.bias_ref, ...), custom_call_target="tpu_custom_call" | custom-call | flops 378535936 | bytes 11829248 | tf_op jit(solution)/shard_map/pallas_call | solution.py:385
  35.7 0.0 copy-done.6
  35.7 0.2 fusion.1
  35.8 0.2 multiply_reduce_fusion.1
  36.1 0.1 add_convert_fusion.1.norm_ref
  36.2 0.0 copy-done.4
  36.2 0.0 copy-done.5
  36.2 48.3 %shard_map.159 = f32[32,2432]{1,0:T(8,128)S(1)} custom-call(bf16[32,2432]{1,0:T(8,128)(2,1)S(1)} %add_convert_fusion.1.norm_ref, bf16[608,2432]{1,0:T(8,128)(2,1)S(1)} %bitcast.27, bf16[608,2432]{1,0:T(8,128)(2,1)S(1)} %copy-done.5), custom_call_target="tpu_custom_call" | custom-call | flops 3028287488 | bytes 5914624 | tf_op jit(solution)/shard_map/pallas_call | solution.py:167
  84.5 0.0 copy-start.7
  84.5 0.2 fusion.2
  84.7 0.2 multiply_reduce_fusion
  85.0 0.0 copy-done
  85.0 0.3 fusion
  85.3 6.7 %collective-permute-start = (f32[32,64]{1,0:T(8,128)S(1)}, f32[32,64]{1,0:T(8,128)S(1)}, u32[]{:S(2)}, u32[]{:S(2)}) collective-permute-start(f32[32,64]{1,0:T(8,128)S(1)} %fusion), channel_id=1, source_target_pairs={{0,16},{16,0},{1,17},{17,1},{2,18},{18,2},{3,19},{19,3},{4,20},{20... | collective-permute-start | bytes 24584 | tf_op jit(solution)/shard_map/ppermute | solution.py:22
  93.4 0.0 collective-permute-done
  93.4 0.0 copy-done.7
  93.4 0.7 multiply_add_fusion.1
  (6 shorter events, 0.0 us)
Async XLA Ops:
  0.6 84.3 %copy-start = (bf16[2432,64]{0,1:T(8,128)(2,1)S(1)}, bf16[2432,64]{0,1:T(8,128)(2,1)}, u32[]{:S(2)}) copy-start(bf16[2432,64]{0,1:T(8,128)(2,1)} %param.25) | copy-start | bytes 933892
  3.2 0.9 copy-start.1
  4.1 0.9 copy-start.2
  5.0 0.9 copy-start.3
  6.0 29.7 %copy-start.6 = (bf16[1,32,2432]{2,1,0:T(8,128)(2,1)S(1)}, bf16[1,32,2432]{2,1,0:T(8,128)(2,1)}, u32[]{:S(2)}) copy-start(bf16[1,32,2432]{2,1,0:T(8,128)(2,1)} %param.20) | copy-start | bytes 466948
  6.0 30.3 %copy-start.4 = (bf16[2432,608]{0,1:T(8,128)(2,1)S(1)}, bf16[2432,608]{0,1:T(8,128)(2,1)}, u32[]{:S(2)}) copy-start(bf16[2432,608]{0,1:T(8,128)(2,1)} %param.23) | copy-start | bytes 8871940
  6.0 30.3 %copy-start.5 = (bf16[608,2432]{1,0:T(8,128)(2,1)S(1)}, bf16[608,2432]{1,0:T(8,128)(2,1)}, u32[]{:S(2)}) copy-start(bf16[608,2432]{1,0:T(8,128)(2,1)} %down_ref.1) | copy-start | bytes 8871940
  84.5 8.9 %copy-start.7 = (f32[32,32]{1,0:T(8,128)S(1)}, f32[32,32]{1,0:T(8,128)}, u32[]{:S(2)}) copy-start(f32[32,32]{1,0:T(8,128)} %param.26) | copy-start | bytes 12292
  85.3 8.1 %collective-permute-start = (f32[32,64]{1,0:T(8,128)S(1)}, f32[32,64]{1,0:T(8,128)S(1)}, u32[]{:S(2)}, u32[]{:S(2)}) collective-permute-start(f32[32,64]{1,0:T(8,128)S(1)} %fusion), channel_id=1, source_target_pairs={{0,16},{16,0},{1,17},{17,1},{2,18},{18,2},{3,19},{19,3},{4,20},{20... | collective-permute-start | bytes 24584 | tf_op jit(solution)/shard_map/ppermute | solution.py:22
